TPU v7x, 32 devices: a whole 2x2x4 slice. The times are simulated.
32 devices in a mesh: row: 4 (over z), col: 2 (over core), rep: 4 (over y, x).
Axes of the slice: x: 2, y: 2, z: 4, core: 2. Of those that a mesh axis runs over, the one named last changes fastest.
Arguments:
- pre_act: bfloat16 [16384, 12288], P(('rep', 'col'), 'row'), may hold values from -8 to 8
- w_out: bfloat16 [12288, 6144], P('row', 'col'), may hold values from -0.0546875 to 0.0546875
- grad_out: bfloat16 [16384, 6144], P(('rep', 'row'), 'col'), may hold values from -6 to 6
Outputs:
- grad_pre: bfloat16 [16384, 12288], P(('rep', 'col'), 'row')
- grad_weight: float32 [12288, 6144], P(('row', 'rep'), 'col')
All inputs are finite; a program needn't handle non-finite values.
Results may differ from a plain program's by a relative error of at most 0.0027.
Values may be sent and summed in bfloat16 or wider, within the bound.
No kernel may reach another device: no remote copies, remote signals or barrier semaphores. Data moves between devices by JAX's collectives and lax.ppermute only.
A program may use at most 256 MiB of HBM per device.

v0:
```python
import jax
import jax.numpy as jnp
from jax import lax
from jax.sharding import PartitionSpec as P

SQRT_TWO_PI = 0.7978845608028654
CUBIC = 0.044715


def gelu_pair(values):
    inner = SQRT_TWO_PI * (values + CUBIC * values * values * values)
    bent = jnp.tanh(inner)
    output = 0.5 * values * (1.0 + bent)
    slopes = 0.5 * (1.0 + bent) + 0.5 * values * (1.0 - bent * bent) * SQRT_TWO_PI * (
        1.0 + 3.0 * CUBIC * values * values
    )
    return (output, slopes)


def contract_rows(left, right):
    return lax.dot_general(
        left, right, (((0,), (0,)), ((), ())), preferred_element_type=jnp.float32
    )


def on_device(pre_act, w_out, grad_out):
    total_tokens = grad_out.shape[0] * lax.axis_size("row") * lax.axis_size("rep")
    factor = float(total_tokens) ** (-0.5)
    grad_all = lax.all_gather(grad_out, "row", axis=0, tiled=True)
    output, slopes = gelu_pair(pre_act.astype(jnp.float32))
    activation = output.astype(jnp.bfloat16)
    block = grad_all
    grad_act = lax.psum_scatter(
        lax.dot_general(block, w_out, (((1,), (1,)), ((), ())), preferred_element_type=jnp.float32),
        "col",
        scatter_dimension=0,
        tiled=True,
    )
    grad_pre = (grad_act * slopes).astype(jnp.bfloat16)
    block = grad_all
    whole = contract_rows(lax.all_gather(activation, "col", axis=0, tiled=True), block)
    grad_weight = lax.psum_scatter(whole * factor, "rep", scatter_dimension=0, tiled=True)
    return (grad_pre, grad_weight)


def solution(mesh):
    in_specs = (P(("rep", "col"), "row"), P("row", "col"), P(("rep", "row"), "col"))
    out_specs = (P(("rep", "col"), "row"), P(("row", "rep"), "col"))
    return jax.shard_map(
        on_device, mesh=mesh, in_specs=in_specs, out_specs=out_specs, check_vma=False
    )
```

profile of v0, /device:TPU:0, one launch (start us, length us, event | category | flops | bytes accessed | tf_op | source)
XLA Modules:
  0.0 1076.4 jit_solution(5641273784048850490)
XLA Ops:
  7.2 0.0 all-gather.3.cloned.1.call-start
  7.2 0.7 all-gather.3.cloned.1.call-update
  7.9 0.0 reduce-scatter.8.cloned.1.call-start
  7.9 429.5 %all-gather.3.cloned.1.call-done = bf16[4096,3072]{1,0:T(8,128)(2,1)} async-done(((bf16[1024,3072]{1,0:T(8,128)(2,1)}), bf16[4096,3072]{1,0:T(8,128)(2,1)}) %all-gather.3.cloned.1.call-update) | async-done | bytes 25165840 | tf_op jit(solution)/shard_map/all_gather | solution.py:29
  437.5 88.2 %fusion.11 = f32[4096,3072]{1,0:T(8,128)} fusion(bf16[4096,3072]{1,0:T(8,128)(2,1)} %all-gather.3.cloned.1.call-done, bf16[3072,3072]{1,0:T(8,128)(2,1)} %param.4), kind=kOutput, calls=%fused_computation.19 | convolution fusion | flops 77309411328 | bytes 94371840 | tf_op jit(solution)/shard_map/dot_general | solution.py:34
  525.6 0.0 reduce-scatter.8.cloned.1.call-update
  525.7 0.0 all-gather.5.cloned.1.call-start
  525.7 61.7 %reduce-scatter.8.cloned.1.call-done = f32[2048,3072]{1,0:T(8,128)} async-done(((f32[4096,3072]{1,0:T(8,128)}), f32[2048,3072]{1,0:T(8,128)}) %reduce-scatter.8.cloned.1.call-update) | async-done | bytes 25165840
  587.4 27.2 %fusion.7 = (bf16[2048,3072]{1,0:T(8,128)(2,1)}, bf16[2048,3072]{1,0:T(8,128)(2,1)}) fusion(bf16[2048,3072]{1,0:T(8,128)(2,1)} %param.3, f32[2048,3072]{1,0:T(8,128)} %reduce-scatter.8.cloned.1.call-done), kind=kLoop, calls=%fused_computation.14 | loop fusion | flops 138412032 | bytes 62914560 | tf_op jit(solution)/shard_map/convert_element_type | solution.py:31
  614.6 0.0 all-gather.5.cloned.1.call-update
  614.7 0.0 reduce-scatter.6.cloned.1.call-start
  614.7 41.5 %all-gather.5.cloned.1.call-done = bf16[4096,3072]{1,0:T(8,128)(2,1)} async-done(((bf16[2048,3072]{1,0:T(8,128)(2,1)}), bf16[4096,3072]{1,0:T(8,128)(2,1)}) %all-gather.5.cloned.1.call-update) | async-done | bytes 25165840 | tf_op jit(solution)/shard_map/all_gather | solution.py:41
  656.2 89.7 %convolution_multiply_fusion = f32[3072,3072]{1,0:T(8,128)} fusion(bf16[4096,3072]{1,0:T(8,128)(2,1)} %all-gather.5.cloned.1.call-done, bf16[4096,3072]{1,0:T(8,128)(2,1)} %all-gather.3.cloned.1.call-done), kind=kOutput, calls=%fused_computation.18 | convolution fusion | flops 77318848512 | bytes 88080384 | tf_op jit(solution)/shard_map/dot_general | solution.py:21
  745.9 0.0 reduce-scatter.6.cloned.1.call-update
  745.9 323.9 %reduce-scatter.6.cloned.1.call-done = f32[768,3072]{1,0:T(8,128)} async-done(((f32[3072,3072]{1,0:T(8,128)}), f32[768,3072]{1,0:T(8,128)}) %reduce-scatter.6.cloned.1.call-update) | async-done | bytes 9437200 | tf_op jit(solution)/shard_map/reduce_scatter | solution.py:42
Async XLA Ops:
  7.2 430.3 %all-gather.3.cloned.1.call-start = ((), (), s32[]{:S(2)}) async-start(), calls=%async_computation.2 | async-start | bytes 31457280 | tf_op jit(solution)/shard_map/all_gather | solution.py:29
  7.9 579.5 %reduce-scatter.8.cloned.1.call-start = ((), (), s32[]{:S(2)}) async-start(), calls=%async_computation.5 | async-start | bytes 75497472
  525.7 130.6 %all-gather.5.cloned.1.call-start = ((), (), s32[]{:S(2)}) async-start(), calls=%async_computation.3 | async-start | bytes 37748736 | tf_op jit(solution)/shard_map/all_gather | solution.py:41
  614.7 455.2 %reduce-scatter.6.cloned.1.call-start = ((), (), s32[]{:S(2)}) async-start(), calls=%async_computation.4 | async-start | bytes 47185920 | tf_op jit(solution)/shard_map/reduce_scatter | solution.py:42
Sparse Core Ops, SparseCore 0:
  9.6 427.8 all-gather.2
  525.8 61.5 reduce-scatter.7
  614.8 41.4 all-gather.4
  746.1 323.7 reduce-scatter.5
where the time goes:
time: 1080 us
  waiting for transfers between devices  857 us (79%)
  matrix products  178 us (16%)
  other arithmetic  27.2 us (3%)
  between operations  13.8 us (1%)
    all_gather x1, waiting for transfers between devices, on_device(): grad_all = lax.all_gather(grad_out, 'row', axis=0, tiled=True)  430 us
    reduce_scatter x1, waiting for transfers between devices, on_device(): lax.psum_scatter(whole * factor, 'rep', scatter_dimension=0, tiled=True)  324 us
    dot_general x1, matrix products, contract_rows(): lax.dot_general(left, right, (((0,), (0,)), ((), ())), preferred_element_...  89.7 us
    dot_general x1, matrix products, on_device(): lax.dot_general(block, w_out, (((1,), (1,)), ((), ())), preferred_element...  88.2 us
    unnamed x5, waiting for transfers between devices  62.4 us
    all_gather x1, waiting for transfers between devices, on_device(): lax.all_gather(activation, 'col', axis=0, tiled=True)  41.5 us
    convert_element_type x1, other arithmetic, on_device(): activation = output.astype(jnp.bfloat16)  27.2 us
  transfers between devices with their start and end apart: 4, of which 4 were waited for; matrix products, arithmetic and copies ran while one was open for 0% of the time, Pallas kernels for 0%

commit v1 on v0

v1 whole, which is shorter than its diff:
```python
import jax
import jax.numpy as jnp
from jax import lax
from jax.sharding import PartitionSpec as P

SQRT_TWO_PI = 0.7978845608028654
CUBIC = 0.044715
WINDOW = 3
RING_LIMIT = 8


def gelu(values):
    inner = SQRT_TWO_PI * (values + CUBIC * values * values * values)
    return 0.5 * values * (1.0 + jnp.tanh(inner))


def gelu_slopes(values):
    inner = SQRT_TWO_PI * (values + CUBIC * values * values * values)
    bent = jnp.tanh(inner)
    return 0.5 * (1.0 + bent) + 0.5 * values * (1.0 - bent * bent) * SQRT_TWO_PI * (
        1.0 + 3.0 * CUBIC * values * values
    )


def contract_rows(left, right):
    return lax.dot_general(
        left, right, (((0,), (0,)), ((), ())), preferred_element_type=jnp.float32
    )


def contract_columns(left, right):
    return lax.dot_general(
        left, right, (((1,), (1,)), ((), ())), preferred_element_type=jnp.float32
    )


def chunk_widths(width):
    unit = 128
    for parts in (12, 8, 6, 4):
        if width % (parts * unit) == 0:
            unit = width // parts
            return [2 * unit] * (parts // 2 - 1) + [unit, unit]
    return [width]


def meet(one, other):
    return lax.optimization_barrier((one, other))[0]


def swap(x, axis, size, step):
    return lax.ppermute(x, axis, [(i, (i + step) % size) for i in range(size)])


def gather_rows(chunks, n, nc):
    row, col = lax.axis_index("row"), lax.axis_index("col")
    shift = col * (n // nc)
    count, rows = len(chunks), chunks[0].shape[0]

    if n > RING_LIMIT:
        out = []
        for chunk in chunks:
            whole = lax.all_gather(chunk, "row", axis=0, tiled=True)
            twice = jnp.concatenate([whole, whole], axis=0)
            out.append(lax.dynamic_slice_in_dim(twice, shift * rows, n * rows, 0))
        return out

    def place(buffer, piece, step):
        slot = (row - step + 2 * n - shift) % n
        return lax.dynamic_update_slice_in_dim(buffer, piece, slot * rows, 0)

    order = [
        (t - s, s) for t in range(count + n - 2) for s in range(n - 1) if 0 <= t - s < count
    ]
    held = list(chunks)
    buffers = [
        place(jnp.zeros((n * rows, c.shape[1]), c.dtype), c, 0) for c in chunks
    ]
    done = []
    for index, (k, s) in enumerate(order):
        source = held[k]
        if index >= WINDOW:
            source = meet(source, done[index - WINDOW])
        held[k] = swap(source, "row", n, 1)
        done.append(held[k])
        buffers[k] = place(buffers[k], held[k], s + 1)
    return buffers


def solution(mesh):
    n, nc, nr = (mesh.shape[axis] for axis in ("row", "col", "rep"))
    pairs = nr & (nr - 1) == 0

    def partner(p, d):
        return p ^ d if pairs else (p + d) % nr

    def on_device(pre_act, w_out, grad_out):
        tokens = grad_out.shape[0] * n * nr
        factor = float(tokens) ** (-0.5)
        rep = lax.axis_index("rep")
        mine_rows, hidden = pre_act.shape
        part = hidden // nr
        widths = chunk_widths(grad_out.shape[1])
        starts = [sum(widths[:k]) for k in range(len(widths))]
        spans = [slice(a, a + b) for a, b in zip(starts, widths)]

        gathered = gather_rows([grad_out[:, span] for span in spans], n, nc)

        acts = []
        for d in range(nr):
            block = lax.dynamic_slice_in_dim(pre_act, partner(rep, d) * part, part, 1)
            own = gelu(block.astype(jnp.float32)).astype(jnp.bfloat16)
            rest = [swap(own, "col", nc, nc - j) for j in range(1, nc)]
            acts.append(jnp.concatenate([own] + rest, axis=0))
        weights = [w_out] + [swap(w_out, "col", nc, nc - j) for j in range(1, nc)]

        grad_act = None
        grad_weight = jnp.zeros((part, grad_out.shape[1]), jnp.float32)
        slopes = gelu_slopes(pre_act.astype(jnp.float32))
        for span, block in zip(spans, gathered):
            features = [block[:mine_rows]]
            for j in range(1, nc):
                other = block[j * mine_rows : (j + 1) * mine_rows]
                features.append(swap(other, "col", nc, j))
            total = None
            arrived = []
            for d in range(nr - 1, 0, -1):
                term = (contract_rows(acts[d], block) * factor).astype(jnp.bfloat16)
                pairs_d = [(p, partner(p, d)) for p in range(nr)]
                arrived.append(lax.ppermute(term, "rep", pairs_d))
            total = contract_rows(acts[0], block) * factor
            left = jnp.concatenate(features, axis=1)
            right = jnp.concatenate([w[:, span] for w in weights], axis=1)
            term = contract_columns(left, right)
            grad_act = term if grad_act is None else grad_act + term
            for other in arrived:
                total = total + other.astype(jnp.float32)
            grad_weight = lax.dynamic_update_slice_in_dim(grad_weight, total, span.start, 1)
        grad_pre = (grad_act * slopes).astype(jnp.bfloat16)
        return grad_pre, grad_weight

    in_specs = (P(("rep", "col"), "row"), P("row", "col"), P(("rep", "row"), "col"))
    out_specs = (P(("rep", "col"), "row"), P(("row", "rep"), "col"))
    return jax.shard_map(
        on_device, mesh=mesh, in_specs=in_specs, out_specs=out_specs, check_vma=False
    )
```

time: 1080 us -> 770 us (0.71)
  waiting for transfers between devices: 857 us -> 190 us
  matrix products: 178 us -> 373 us
  local copies, waits for them, and re-layouts: 0 us -> 121 us
  starting transfers between devices: 0.16 us -> 53.2 us
  between operations: 13.8 us -> 1.57 us
    all_gather x2 -> x0, waiting for transfers between devices: 471 us -> none  [the longest x1 430 us: on_device(): grad_all = lax.all_gather(grad_out, 'row', axis=0, tiled=True)]
    reduce_scatter x1 -> x0, waiting for transfers between devices: 324 us -> none  [on_device(): lax.psum_scatter(whole * factor, 'rep', scatter_dimension=0, tiled=True)]
    ppermute x0 -> x54, waiting for transfers between devices: none -> 190 us  [the longest x33 142 us: swap(): return lax.ppermute(x, axis, [(i, (i + step) % size) for i in range(size)])]
    dot_general x1 -> x28, matrix products: 89.7 us -> 198 us  [contract_rows(): lax.dot_general(left, right, (((0,), (0,)), ((), ())), preferred_element_...]
    dot_general x1 -> x7, matrix products: 88.2 us -> 175 us  [contract_columns(): lax.dot_general(left, right, (((1,), (1,)), ((), ())), preferred_element_...]
    unnamed x5 -> x0, waiting for transfers between devices: 62.4 us -> none
    slice x0 -> x12, local copies, waits for them, and re-layouts: none -> 60.1 us  [the longest x4 32.1 us: on_device(): right = jnp.concatenate([w[:, span] for w in weights], axis=1)]
    ppermute x0 -> x54, starting transfers between devices: none -> 53.2 us  [the longest x21 26.9 us: on_device(): arrived.append(lax.ppermute(term, 'rep', pairs_d))]
  transfers between devices with their start and end apart: 4 -> 54, of which waited for: 4 -> 19; matrix products, arithmetic and copies ran while one was open for 0% -> 59% of each run, Pallas kernels for 0% -> 0%
where the time goes in v1:
time: 770 us; the launch traced here: 761 us
  matrix products  373 us (48%)
  waiting for transfers between devices  190 us (25%)
  local copies, waits for them, and re-layouts  121 us (16%)
  starting transfers between devices  53.2 us (7%)
  other arithmetic  21.5 us (3%)
    dot_general x28, matrix products, contract_rows(): lax.dot_general(left, right, (((0,), (0,)), ((), ())), preferred_element_...  198 us
    dot_general x7, matrix products, contract_columns(): lax.dot_general(left, right, (((1,), (1,)), ((), ())), preferred_element_...  175 us
    ppermute x33, waiting for transfers between devices, swap(): return lax.ppermute(x, axis, [(i, (i + step) % size) for i in range(size)])  142 us
    ppermute x21, waiting for transfers between devices, on_device(): arrived.append(lax.ppermute(term, 'rep', pairs_d))  48.2 us
    dynamic_update_slice x27, local copies, waits for them, and re-layouts, place(): return lax.dynamic_update_slice_in_dim(buffer, piece, slot * rows, 0)  45.3 us
    slice x4, local copies, waits for them, and re-layouts, on_device(): right = jnp.concatenate([w[:, span] for w in weights], axis=1)  32.1 us
    ppermute x21, starting transfers between devices, on_device(): arrived.append(lax.ppermute(term, 'rep', pairs_d))  26.9 us
    slice x7, local copies, waits for them, and re-layouts, on_device(): features = [block[:mine_rows]]  26.8 us
  transfers between devices with their start and end apart: 54, of which 19 were waited for; matrix products, arithmetic and copies ran while one was open for 59% of the time, Pallas kernels for 0%

profile of v1, /device:TPU:0, one launch (start us, length us, event | category | flops | bytes accessed | tf_op | source)
XLA Modules:
  0.0 760.8 jit_solution(5951040149170894630)
XLA Ops:
  2.9 5.2 constant_dynamic-update-slice_fusion.23
  8.1 3.0 collective-permute-start.5
  12.7 13.5 %fusion.10 = (bf16[2048,768]{1,0:T(8,128)(2,1)}, bf16[2048,768]{1,0:T(8,128)(2,1)}, bf16[2048,768]{1,0:T(8,128)(2,1)}, bf16[2048,768]{1,0:T(8,128)(2,1)}) fusion(bf16[2048,3072]{1,0:T(8,128)(2,1)} %param.3, s32[]{:T(128)S(6)} %select_n.123, s32[]{:T(128)S(6)} %select_n.124, s32[]{:T(128)S(6)} %select_n.126, s32[]{:T(128)S(6)} %select_n.125), kind=kLoop, calls=%fused_computation.37 | loop fusion | flops 62914560 | bytes 25165840 | tf_op jit(solution)/shard_map/convert_element_type | solution.py:111
  36.3 11.6 %fusion.108 = (bf16[3072,512]{1,0:T(8,128)(2,1)}, bf16[3072,512]{1,0:T(8,128)(2,1)}, bf16[3072,512]{1,0:T(8,128)(2,1)}, bf16[3072,512]{1,0:T(8,128)(2,1)}, bf16[3072,512]{1,0:T(8,128)(2,1)}) fusion(bf16[3072,3072]{1,0:T(8,128)(2,1)} %param.4), kind=kLoop, calls=%fused_computation.193 | loop fusion | bytes 31457280 | tf_op jit(solution)/shard_map/slice | solution.py:132
  49.5 10.4 %collective-permute-done = bf16[1024,512]{1,0:T(8,128)(2,1)} collective-permute-done((bf16[1024,512]{1,0:T(8,128)(2,1)}, bf16[1024,512]{1,0:T(8,128)(2,1)}, u32[]{:S(2)}, u32[]{:S(2)}) %collective-permute-start) | collective-permute-done | bytes 1048608 | tf_op jit(solution)/shard_map/ppermute | solution.py:51
  62.1 3.7 fusion.106
  65.8 16.5 %collective-permute-done.6 = bf16[1024,512]{1,0:T(8,128)(2,1)S(1)} collective-permute-done((bf16[1024,512]{1,0:T(8,128)(2,1)}, bf16[1024,512]{1,0:T(8,128)(2,1)S(1)}, u32[]{:S(2)}, u32[]{:S(2)}) %collective-permute-start.6) | collective-permute-done | bytes 1048608 | tf_op jit(solution)/shard_map/ppermute | solution.py:51
  82.3 22.6 %collective-permute-done.9 = bf16[1024,512]{1,0:T(8,128)(2,1)} collective-permute-done((bf16[1024,512]{1,0:T(8,128)(2,1)S(1)}, bf16[1024,512]{1,0:T(8,128)(2,1)}, u32[]{:S(2)}, u32[]{:S(2)}) %collective-permute-start.9) | collective-permute-done | bytes 1048608 | tf_op jit(solution)/shard_map/ppermute | solution.py:51
  110.0 17.4 %collective-permute-done.1 = bf16[1024,512]{1,0:T(8,128)(2,1)} collective-permute-done((bf16[1024,512]{1,0:T(8,128)(2,1)}, bf16[1024,512]{1,0:T(8,128)(2,1)}, u32[]{:S(2)}, u32[]{:S(2)}) %collective-permute-start.1) | collective-permute-done | bytes 1048608 | tf_op jit(solution)/shard_map/ppermute | solution.py:51
  141.3 8.5 %collective-permute-done.10 = bf16[1024,512]{1,0:T(8,128)(2,1)} collective-permute-done((bf16[1024,512]{1,0:T(8,128)(2,1)}, bf16[1024,512]{1,0:T(8,128)(2,1)}, u32[]{:S(2)}, u32[]{:S(2)}) %collective-permute-start.10) | collective-permute-done | bytes 1048608 | tf_op jit(solution)/shard_map/ppermute | solution.py:51
  152.2 20.0 %collective-permute-done.13 = bf16[1024,512]{1,0:T(8,128)(2,1)S(1)} collective-permute-done((bf16[1024,512]{1,0:T(8,128)(2,1)}, bf16[1024,512]{1,0:T(8,128)(2,1)S(1)}, u32[]{:S(2)}, u32[]{:S(2)}) %collective-permute-start.13) | collective-permute-done | bytes 1048608 | tf_op jit(solution)/shard_map/ppermute | solution.py:51
  172.2 21.6 %collective-permute-done.2 = bf16[1024,512]{1,0:T(8,128)(2,1)S(1)} collective-permute-done((bf16[1024,512]{1,0:T(8,128)(2,1)}, bf16[1024,512]{1,0:T(8,128)(2,1)S(1)}, u32[]{:S(2)}, u32[]{:S(2)}) %collective-permute-start.2) | collective-permute-done | bytes 1048608 | tf_op jit(solution)/shard_map/ppermute | solution.py:51
  196.0 4.5 fusion.112
  201.8 7.5 multiply_convert_fusion.14
  211.1 7.5 multiply_convert_fusion.12
  221.1 5.6 multiply_convert_fusion.13
  227.3 12.7 %collective-permute-done.31 = bf16[768,512]{1,0:T(8,128)(2,1)S(1)} collective-permute-done((bf16[768,512]{1,0:T(8,128)(2,1)S(1)}, bf16[768,512]{1,0:T(8,128)(2,1)S(1)}, u32[]{:S(2)}, u32[]{:S(2)}) %collective-permute-start.31) | collective-permute-done | bytes 786464 | tf_op jit(solution)/shard_map/ppermute | solution.py:129
  241.5 5.6 fusion.105
  247.2 6.9 collective-permute-done.35
  259.8 6.9 collective-permute-done.7
  268.1 8.5 %multiply_convert_fusion.11 = bf16[768,512]{1,0:T(8,128)(2,1)} fusion(bf16[4096,512]{1,0:T(8,128)(2,1)} %constant_dynamic-update-slice_fusion.20, bf16[2048,768]{1,0:T(8,128)(2,1)} %collective-permute-done.30, bf16[2048,768]{1,0:T(8,128)(2,1)} %get-tuple-element.53), kind=kOutput, calls=%fused_computation.124 | convolution fusion | flops 3234594816 | bytes 11272192 | tf_op jit(solution)/shard_map/dot_general | solution.py:26
  279.0 8.4 %multiply_convert_fusion.9 = bf16[768,512]{1,0:T(8,128)(2,1)} fusion(bf16[4096,512]{1,0:T(8,128)(2,1)} %constant_dynamic-update-slice_fusion.20, bf16[2048,768]{1,0:T(8,128)(2,1)} %collective-permute-done.34, bf16[2048,768]{1,0:T(8,128)(2,1)} %get-tuple-element.54), kind=kOutput, calls=%fused_computation.122 | convolution fusion | flops 3234594816 | bytes 11272192 | tf_op jit(solution)/shard_map/dot_general | solution.py:26
  288.0 6.5 multiply_convert_fusion.10
  294.5 7.9 %fusion.104 = f32[768,512]{1,0:T(8,128)} fusion(bf16[4096,512]{1,0:T(8,128)(2,1)} %constant_dynamic-update-slice_fusion.20, bf16[2048,768]{1,0:T(8,128)(2,1)} %copy-done.24, bf16[2048,768]{1,0:T(8,128)(2,1)S(1)} %copy-done.3), kind=kOutput, calls=%fused_computation.189 | convolution fusion | flops 3233808384 | bytes 12058624 | tf_op jit(solution)/shard_map/dot_general | solution.py:26
  303.0 4.8 fusion.111
  312.2 5.5 collective-permute-done.37
  319.5 13.0 %collective-permute-done.25 = bf16[1024,256]{1,0:T(8,128)(2,1)} collective-permute-done((bf16[1024,256]{1,0:T(8,128)(2,1)S(1)}, bf16[1024,256]{1,0:T(8,128)(2,1)}, u32[]{:S(2)}, u32[]{:S(2)}) %collective-permute-start.25) | collective-permute-done | bytes 524320 | tf_op jit(solution)/shard_map/ppermute | solution.py:51
  336.8 8.4 %multiply_convert_fusion.8 = bf16[768,512]{1,0:T(8,128)(2,1)} fusion(bf16[4096,512]{1,0:T(8,128)(2,1)} %constant_dynamic-update-slice_fusion.16, bf16[2048,768]{1,0:T(8,128)(2,1)} %collective-permute-done.30, bf16[2048,768]{1,0:T(8,128)(2,1)} %get-tuple-element.53), kind=kOutput, calls=%fused_computation.120 | convolution fusion | flops 3234594816 | bytes 11272192 | tf_op jit(solution)/shard_map/dot_general | solution.py:26
  347.4 8.4 %multiply_convert_fusion.6 = bf16[768,512]{1,0:T(8,128)(2,1)} fusion(bf16[4096,512]{1,0:T(8,128)(2,1)} %constant_dynamic-update-slice_fusion.16, bf16[2048,768]{1,0:T(8,128)(2,1)} %collective-permute-done.34, bf16[2048,768]{1,0:T(8,128)(2,1)} %get-tuple-element.54), kind=kOutput, calls=%fused_computation.118 | convolution fusion | flops 3234594816 | bytes 11272192 | tf_op jit(solution)/shard_map/dot_general | solution.py:26
  356.3 8.4 %multiply_convert_fusion.7 = bf16[768,512]{1,0:T(8,128)(2,1)} fusion(bf16[4096,512]{1,0:T(8,128)(2,1)} %constant_dynamic-update-slice_fusion.16, bf16[2048,768]{1,0:T(8,128)(2,1)} %copy-done.25, bf16[2048,768]{1,0:T(8,128)(2,1)} %get-tuple-element.55), kind=kOutput, calls=%fused_computation.119 | convolution fusion | flops 3234594816 | bytes 11272192 | tf_op jit(solution)/shard_map/dot_general | solution.py:26
  364.7 8.6 %fusion.103 = f32[768,512]{1,0:T(8,128)} fusion(bf16[4096,512]{1,0:T(8,128)(2,1)} %constant_dynamic-update-slice_fusion.16, bf16[2048,768]{1,0:T(8,128)(2,1)} %copy-done.24, bf16[2048,768]{1,0:T(8,128)(2,1)} %get-tuple-element.52), kind=kOutput, calls=%fused_computation.188 | convolution fusion | flops 3233808384 | bytes 12058624 | tf_op jit(solution)/shard_map/dot_general | solution.py:26
  374.1 4.5 fusion.113
  384.6 4.3 collective-permute-start.15
  392.4 4.5 collective-permute-done.23
  397.8 6.0 fusion.88
  403.8 6.0 fusion.90
  409.8 3.2 fusion.117
  413.0 5.1 fusion.89
  421.6 8.4 %multiply_convert_fusion.5 = bf16[768,512]{1,0:T(8,128)(2,1)} fusion(bf16[4096,512]{1,0:T(8,128)(2,1)} %constant_dynamic-update-slice_fusion.12, bf16[2048,768]{1,0:T(8,128)(2,1)} %collective-permute-done.30, bf16[2048,768]{1,0:T(8,128)(2,1)} %get-tuple-element.53), kind=kOutput, calls=%fused_computation.116 | convolution fusion | flops 3234594816 | bytes 11272192 | tf_op jit(solution)/shard_map/dot_general | solution.py:26
  432.2 8.4 %multiply_convert_fusion.3 = bf16[768,512]{1,0:T(8,128)(2,1)} fusion(bf16[4096,512]{1,0:T(8,128)(2,1)} %constant_dynamic-update-slice_fusion.12, bf16[2048,768]{1,0:T(8,128)(2,1)} %collective-permute-done.34, bf16[2048,768]{1,0:T(8,128)(2,1)} %get-tuple-element.54), kind=kOutput, calls=%fused_computation.114 | convolution fusion | flops 3234594816 | bytes 11272192 | tf_op jit(solution)/shard_map/dot_general | solution.py:26
  441.1 8.4 %multiply_convert_fusion.4 = bf16[768,512]{1,0:T(8,128)(2,1)} fusion(bf16[4096,512]{1,0:T(8,128)(2,1)} %constant_dynamic-update-slice_fusion.12, bf16[2048,768]{1,0:T(8,128)(2,1)} %copy-done.25, bf16[2048,768]{1,0:T(8,128)(2,1)} %get-tuple-element.55), kind=kOutput, calls=%fused_computation.115 | convolution fusion | flops 3234594816 | bytes 11272192 | tf_op jit(solution)/shard_map/dot_general | solution.py:26
  450.2 8.6 %fusion.102 = f32[768,512]{1,0:T(8,128)} fusion(bf16[4096,512]{1,0:T(8,128)(2,1)} %constant_dynamic-update-slice_fusion.12, bf16[2048,768]{1,0:T(8,128)(2,1)} %copy-done.24, bf16[2048,768]{1,0:T(8,128)(2,1)} %get-tuple-element.52), kind=kOutput, calls=%fused_computation.187 | convolution fusion | flops 3233808384 | bytes 12058624 | tf_op jit(solution)/shard_map/dot_general | solution.py:26
  458.8 4.6 fusion.114
  465.6 8.1 %collective-permute-done.43 = bf16[768,512]{1,0:T(8,128)(2,1)} collective-permute-done((bf16[768,512]{1,0:T(8,128)(2,1)}, bf16[768,512]{1,0:T(8,128)(2,1)}, u32[]{:S(2)}, u32[]{:S(2)}) %collective-permute-start.43) | collective-permute-done | bytes 786464 | tf_op jit(solution)/shard_map/ppermute | solution.py:129
  478.0 7.2 multiply_convert_fusion.2
  487.1 7.2 multiply_convert_fusion
  494.6 7.4 fusion.101
  502.0 7.2 multiply_convert_fusion.1
  514.6 6.1 fusion.91
  520.6 6.5 fusion.93
  527.1 5.3 fusion.92
  535.0 3.0 fusion.116
  544.1 4.6 fusion.85
  548.8 4.2 collective-permute-done.51
  552.9 7.3 collective-permute-done.53
  560.9 4.6 fusion.87
  566.1 14.4 %fusion.109 = (bf16[3072,512]{1,0:T(8,128)(2,1)}, bf16[3072,512]{1,0:T(8,128)(2,1)}, bf16[3072,512]{1,0:T(8,128)(2,1)}, bf16[3072,512]{1,0:T(8,128)(2,1)}, bf16[3072,512]{1,0:T(8,128)(2,1)}) fusion(bf16[3072,3072]{1,0:T(8,128)(2,1)} %collective-permute-done.4), kind=kLoop, calls=%fused_computation.194 | loop fusion | bytes 31457280 | tf_op jit(solution)/shard_map/slice | solution.py:132
  581.2 21.2 %fusion.33 = f32[2048,3072]{1,0:T(8,128)} fusion(bf16[3072,512]{1,0:T(8,128)(2,1)} %get-tuple-element.47, bf16[3072,512]{1,0:T(8,128)(2,1)} %get-tuple-element.42, bf16[2048,512]{1,0:T(8,128)(2,1)} %collective-permute-done.8, bf16[2048,512]{1,0:T(8,128)(2,1)} %get-tuple-element.65), kind=kOutput, calls=%fused_computation.60 | convolution fusion | flops 12905873408 | bytes 35651584 | tf_op jit(solution)/shard_map/dot_general | solution.py:32
  603.7 21.6 %fusion.45 = f32[2048,3072]{1,0:T(8,128)} fusion(bf16[3072,512]{1,0:T(8,128)(2,1)} %get-tuple-element.48, bf16[3072,512]{1,0:T(8,128)(2,1)} %get-tuple-element.43, bf16[2048,512]{1,0:T(8,128)(2,1)} %copy-done.26, bf16[2048,512]{1,0:T(8,128)(2,1)} %get-tuple-element.73), kind=kOutput, calls=%fused_computation.72 | convolution fusion | flops 12905873408 | bytes 35651584 | tf_op jit(solution)/shard_map/dot_general | solution.py:32
  625.3 19.9 %fusion.41 = f32[2048,3072]{1,0:T(8,128)} fusion(bf16[3072,512]{1,0:T(8,128)(2,1)} %get-tuple-element.49, bf16[3072,512]{1,0:T(8,128)(2,1)S(1)} %copy-done.9, bf16[2048,512]{1,0:T(8,128)(2,1)} %collective-permute-done.16, bf16[2048,512]{1,0:T(8,128)(2,1)} %get-tuple-element.71), kind=kOutput, calls=%fused_computation.68 | convolution fusion | flops 12905873408 | bytes 35651584 | tf_op jit(solution)/shard_map/dot_general | solution.py:32
  645.1 21.6 %fusion.37 = f32[2048,3072]{1,0:T(8,128)} fusion(bf16[3072,512]{1,0:T(8,128)(2,1)} %get-tuple-element.50, bf16[3072,512]{1,0:T(8,128)(2,1)} %get-tuple-element.45, bf16[2048,512]{1,0:T(8,128)(2,1)} %collective-permute-done.12, bf16[2048,512]{1,0:T(8,128)(2,1)} %get-tuple-element.69), kind=kOutput, calls=%fused_computation.64 | convolution fusion | flops 12905873408 | bytes 35651584 | tf_op jit(solution)/shard_map/dot_general | solution.py:32
  666.7 19.8 %fusion.29 = f32[2048,3072]{1,0:T(8,128)} fusion(bf16[3072,512]{1,0:T(8,128)(2,1)} %get-tuple-element.51, bf16[3072,512]{1,0:T(8,128)(2,1)S(1)} %copy-done.8, bf16[2048,512]{1,0:T(8,128)(2,1)} %collective-permute-done.3, bf16[2048,512]{1,0:T(8,128)(2,1)} %get-tuple-element.67), kind=kOutput, calls=%fused_computation.56 | convolution fusion | flops 12905873408 | bytes 35651584 | tf_op jit(solution)/shard_map/dot_general | solution.py:32
  689.2 13.4 %fusion.64 = f32[2048,3072]{1,0:T(8,128)} fusion(bf16[3072,256]{1,0:T(8,128)(2,1)S(1)} %get-tuple-element.41, bf16[3072,256]{1,0:T(8,128)(2,1)S(1)} %copy-done.12, bf16[2048,256]{1,0:T(8,128)(2,1)} %collective-permute-done.24, bf16[2048,256]{1,0:T(8,128)(2,1)S(1)} %copy-done.22), kind=kOutput, calls=%fused_computation.95 | convolution fusion | flops 6452936704 | bytes 30408704 | tf_op jit(solution)/shard_map/dot_general | solution.py:32
  702.6 57.8 %fusion.7 = bf16[2048,3072]{1,0:T(8,128)(2,1)} fusion(bf16[2048,3072]{1,0:T(8,128)(2,1)} %param.3, f32[2048,3072]{1,0:T(8,128)} %fusion.64, f32[2048,3072]{1,0:T(8,128)} %fusion.45, f32[2048,3072]{1,0:T(8,128)} %fusion.41, f32[2048,3072]{1,0:T(8,128)} %fusion.37, f32[2048,3072]{1,0:T(8,128)} %fusion.29, f32[2048,3072]{1,0:T(8,128)} %fusion.33, ...), kind=kOutput, calls=%fused_computation.14 | convolution fusion | flops 6616514560 | bytes 181403648 | tf_op jit(solution)/shard_map/dot_general | solution.py:32
  (210 shorter events, 119.4 us)
Async XLA Ops:
  2.9 25.4 %slice-start = ((s8[6291456]{0:T(1024)(128)(4,1)}), s8[2097152]{0:T(1024)(128)(4,1)S(1)}, s32[]{:S(2)}) async-start(s8[6291456]{0:T(1024)(128)(4,1)} %bitcast.28), calls=%async_computation | async-start | bytes 4194304
  8.1 39.8 %collective-permute-start.5 = (bf16[1024,512]{1,0:T(8,128)(2,1)}, bf16[1024,512]{1,0:T(8,128)(2,1)}, u32[]{:S(2)}, u32[]{:S(2)}) collective-permute-start(bf16[1024,512]{1,0:T(8,128)(2,1)} %get-tuple-element.63), channel_id=1, source_target_pairs={{0,8},{8,16},{16,24},{24,0},{1,9},{9,17},{17,25},{25,1},{2,10},{10... | collective-permute-start | bytes 3145736 | tf_op jit(solution)/shard_map/ppermute | solution.py:51
  11.2 48.8 %collective-permute-start = (bf16[1024,512]{1,0:T(8,128)(2,1)}, bf16[1024,512]{1,0:T(8,128)(2,1)}, u32[]{:S(2)}, u32[]{:S(2)}) collective-permute-start(bf16[1024,512]{1,0:T(8,128)(2,1)} %get-tuple-element.64), channel_id=1, source_target_pairs={{0,8},{8,16},{16,24},{24,0},{1,9},{9,17},{17,25},{25,1},{2,10},{10... | collective-permute-start | bytes 3145736 | tf_op jit(solution)/shard_map/ppermute | solution.py:51
  26.3 174.2 %collective-permute-start.30 = (bf16[2048,768]{1,0:T(8,128)(2,1)}, bf16[2048,768]{1,0:T(8,128)(2,1)}, u32[]{:S(2)}, u32[]{:S(2)}) collective-permute-start(bf16[2048,768]{1,0:T(8,128)(2,1)} %get-tuple-element.53), channel_id=1, source_target_pairs={{0,4},{4,0},{1,5},{5,1},{2,6},{6,2},{3,7},{7,3},{8,12},{12,8},{9,1... | collective-permute-start | bytes 9437192 | tf_op jit(solution)/shard_map/ppermute | solution.py:51
  26.3 183.0 %collective-permute-start.34 = (bf16[2048,768]{1,0:T(8,128)(2,1)}, bf16[2048,768]{1,0:T(8,128)(2,1)}, u32[]{:S(2)}, u32[]{:S(2)}) collective-permute-start(bf16[2048,768]{1,0:T(8,128)(2,1)} %get-tuple-element.54), channel_id=1, source_target_pairs={{0,4},{4,0},{1,5},{5,1},{2,6},{6,2},{3,7},{7,3},{8,12},{12,8},{9,1... | collective-permute-start | bytes 9437192 | tf_op jit(solution)/shard_map/ppermute | solution.py:51
  36.3 23.7 %copy-start.17 = (bf16[1024,512]{1,0:T(8,128)(2,1)S(1)}, bf16[1024,512]{1,0:T(8,128)(2,1)}, u32[]{:S(2)}) copy-start(bf16[1024,512]{1,0:T(8,128)(2,1)} %get-tuple-element.23) | copy-start | bytes 3145732
  47.9 34.4 %collective-permute-start.6 = (bf16[1024,512]{1,0:T(8,128)(2,1)}, bf16[1024,512]{1,0:T(8,128)(2,1)S(1)}, u32[]{:S(2)}, u32[]{:S(2)}) collective-permute-start(bf16[1024,512]{1,0:T(8,128)(2,1)} %collective-permute-done.5), channel_id=1, source_target_pairs={{0,8},{8,16},{16,24},{24,0},{1,9},{9,17},{17,25},{25,1},{2,10},{10... | collective-permute-start | bytes 3145736 | tf_op jit(solution)/shard_map/ppermute | solution.py:51
  60.0 44.9 %collective-permute-start.9 = (bf16[1024,512]{1,0:T(8,128)(2,1)S(1)}, bf16[1024,512]{1,0:T(8,128)(2,1)}, u32[]{:S(2)}, u32[]{:S(2)}) collective-permute-start(bf16[1024,512]{1,0:T(8,128)(2,1)S(1)} %copy-done.17), channel_id=1, source_target_pairs={{0,8},{8,16},{16,24},{24,0},{1,9},{9,17},{17,25},{25,1},{2,10},{10... | collective-permute-start | bytes 3145736 | tf_op jit(solution)/shard_map/ppermute | solution.py:51
  60.4 46.9 %copy-start = (bf16[4096,512]{1,0:T(8,128)(2,1)}, bf16[4096,512]{1,0:T(8,128)(2,1)S(1)}, u32[]{:S(2)}) copy-start(bf16[4096,512]{1,0:T(8,128)(2,1)S(1)} %constant_dynamic-update-slice_fusion.11) | copy-start | bytes 12582916
  60.5 66.9 %collective-permute-start.1 = (bf16[1024,512]{1,0:T(8,128)(2,1)}, bf16[1024,512]{1,0:T(8,128)(2,1)}, u32[]{:S(2)}, u32[]{:S(2)}) collective-permute-start(bf16[1024,512]{1,0:T(8,128)(2,1)} %collective-permute-done), channel_id=1, source_target_pairs={{0,8},{8,16},{16,24},{24,0},{1,9},{9,17},{17,25},{25,1},{2,10},{10... | collective-permute-start | bytes 3145736 | tf_op jit(solution)/shard_map/ppermute | solution.py:51
  82.3 22.6 %copy-start.18 = (bf16[1024,512]{1,0:T(8,128)(2,1)}, bf16[1024,512]{1,0:T(8,128)(2,1)S(1)}, u32[]{:S(2)}) copy-start(bf16[1024,512]{1,0:T(8,128)(2,1)S(1)} %collective-permute-done.6) | copy-start | bytes 3145732
  104.9 44.9 %collective-permute-start.10 = (bf16[1024,512]{1,0:T(8,128)(2,1)}, bf16[1024,512]{1,0:T(8,128)(2,1)}, u32[]{:S(2)}, u32[]{:S(2)}) collective-permute-start(bf16[1024,512]{1,0:T(8,128)(2,1)} %collective-permute-done.9), channel_id=1, source_target_pairs={{0,8},{8,16},{16,24},{24,0},{1,9},{9,17},{17,25},{25,1},{2,10},{10... | collective-permute-start | bytes 3145736 | tf_op jit(solution)/shard_map/ppermute | solution.py:51
  108.4 63.8 %collective-permute-start.13 = (bf16[1024,512]{1,0:T(8,128)(2,1)}, bf16[1024,512]{1,0:T(8,128)(2,1)S(1)}, u32[]{:S(2)}, u32[]{:S(2)}) collective-permute-start(bf16[1024,512]{1,0:T(8,128)(2,1)} %get-tuple-element.26), channel_id=1, source_target_pairs={{0,8},{8,16},{16,24},{24,0},{1,9},{9,17},{17,25},{25,1},{2,10},{10... | collective-permute-start | bytes 3145736 | tf_op jit(solution)/shard_map/ppermute | solution.py:51
  127.4 66.5 %collective-permute-start.2 = (bf16[1024,512]{1,0:T(8,128)(2,1)}, bf16[1024,512]{1,0:T(8,128)(2,1)S(1)}, u32[]{:S(2)}, u32[]{:S(2)}) collective-permute-start(bf16[1024,512]{1,0:T(8,128)(2,1)} %collective-permute-done.1), channel_id=1, source_target_pairs={{0,8},{8,16},{16,24},{24,0},{1,9},{9,17},{17,25},{25,1},{2,10},{10... | collective-permute-start | bytes 3145736 | tf_op jit(solution)/shard_map/ppermute | solution.py:51
  135.5 36.7 %copy-start.3 = (bf16[2048,768]{1,0:T(8,128)(2,1)S(1)}, bf16[2048,768]{1,0:T(8,128)(2,1)}, u32[]{:S(2)}) copy-start(bf16[2048,768]{1,0:T(8,128)(2,1)} %get-tuple-element.52) | copy-start | bytes 9437188
  149.9 68.7 %collective-permute-start.32 = (bf16[2048,768]{1,0:T(8,128)(2,1)S(1)}, bf16[2048,768]{1,0:T(8,128)(2,1)S(1)}, u32[]{:S(2)}, u32[]{:S(2)}) collective-permute-start(bf16[2048,768]{1,0:T(8,128)(2,1)S(1)} %copy-done.5), channel_id=1, source_target_pairs={{0,4},{4,0},{1,5},{5,1},{2,6},{6,2},{3,7},{7,3},{8,12},{12,8},{9,1... | collective-permute-start | bytes 9437192 | tf_op jit(solution)/shard_map/ppermute | solution.py:51
  172.2 54.5 %collective-permute-start.29 = (bf16[2048,768]{1,0:T(8,128)(2,1)S(1)}, bf16[2048,768]{1,0:T(8,128)(2,1)S(1)}, u32[]{:S(2)}, u32[]{:S(2)}) collective-permute-start(bf16[2048,768]{1,0:T(8,128)(2,1)S(1)} %copy-done.3), channel_id=1, source_target_pairs={{0,4},{4,0},{1,5},{5,1},{2,6},{6,2},{3,7},{7,3},{8,12},{12,8},{9,1... | collective-permute-start | bytes 9437192 | tf_op jit(solution)/shard_map/ppermute | solution.py:51
  193.9 63.1 %collective-permute-start.14 = (bf16[1024,512]{1,0:T(8,128)(2,1)S(1)}, bf16[1024,512]{1,0:T(8,128)(2,1)S(1)}, u32[]{:S(2)}, u32[]{:S(2)}) collective-permute-start(bf16[1024,512]{1,0:T(8,128)(2,1)S(1)} %collective-permute-done.13), channel_id=1, source_target_pairs={{0,8},{8,16},{16,24},{24,0},{1,9},{9,17},{17,25},{25,1},{2,10},{10... | collective-permute-start | bytes 3145736 | tf_op jit(solution)/shard_map/ppermute | solution.py:51
  200.5 56.5 %collective-permute-start.17 = (bf16[1024,512]{1,0:T(8,128)(2,1)S(1)}, bf16[1024,512]{1,0:T(8,128)(2,1)}, u32[]{:S(2)}, u32[]{:S(2)}) collective-permute-start(bf16[1024,512]{1,0:T(8,128)(2,1)S(1)} %get-tuple-element.29), channel_id=1, source_target_pairs={{0,8},{8,16},{16,24},{24,0},{1,9},{9,17},{17,25},{25,1},{2,10},{10... | collective-permute-start | bytes 3145736 | tf_op jit(solution)/shard_map/ppermute | solution.py:51
  209.3 57.4 %collective-permute-start.7 = (bf16[1024,512]{1,0:T(8,128)(2,1)S(1)}, bf16[1024,512]{1,0:T(8,128)(2,1)S(1)}, u32[]{:S(2)}, u32[]{:S(2)}) collective-permute-start(bf16[1024,512]{1,0:T(8,128)(2,1)S(1)} %copy-done.19), channel_id=1, source_target_pairs={{0,8},{8,16},{16,24},{24,0},{1,9},{9,17},{17,25},{25,1},{2,10},{10... | collective-permute-start | bytes 3145736 | tf_op jit(solution)/shard_map/ppermute | solution.py:51
  218.6 69.4 %copy-start.25 = (bf16[2048,768]{1,0:T(8,128)(2,1)}, bf16[2048,768]{1,0:T(8,128)(2,1)S(1)}, u32[]{:S(2)}) copy-start(bf16[2048,768]{1,0:T(8,128)(2,1)S(1)} %collective-permute-done.32) | copy-start | bytes 9437188
  218.6 21.4 %collective-permute-start.31 = (bf16[768,512]{1,0:T(8,128)(2,1)S(1)}, bf16[768,512]{1,0:T(8,128)(2,1)S(1)}, u32[]{:S(2)}, u32[]{:S(2)}) collective-permute-start(bf16[768,512]{1,0:T(8,128)(2,1)S(1)} %multiply_convert_fusion.14), channel_id=1, source_target_pairs={{0,3},{1,2},{2,1},{3,0},{4,7},{5,6},{6,5},{7,4},{8,11},{9,10},{10,... | collective-permute-start | bytes 2359304 | tf_op jit(solution)/shard_map/ppermute | solution.py:129
  226.7 20.4 %copy-start.24 = (bf16[2048,768]{1,0:T(8,128)(2,1)}, bf16[2048,768]{1,0:T(8,128)(2,1)S(1)}, u32[]{:S(2)}) copy-start(bf16[2048,768]{1,0:T(8,128)(2,1)S(1)} %collective-permute-done.29) | copy-start | bytes 9437188
  226.7 27.3 %collective-permute-start.35 = (bf16[768,512]{1,0:T(8,128)(2,1)S(1)}, bf16[768,512]{1,0:T(8,128)(2,1)S(1)}, u32[]{:S(2)}, u32[]{:S(2)}) collective-permute-start(bf16[768,512]{1,0:T(8,128)(2,1)S(1)} %multiply_convert_fusion.12), channel_id=1, source_target_pairs={{0,1},{1,0},{2,3},{3,2},{4,5},{5,4},{6,7},{7,6},{8,9},{9,8},{10,11... | collective-permute-start | bytes 2359304 | tf_op jit(solution)/shard_map/ppermute | solution.py:129
  240.0 15.4 %collective-permute-start.33 = (bf16[768,512]{1,0:T(8,128)(2,1)S(1)}, bf16[768,512]{1,0:T(8,128)(2,1)S(1)}, u32[]{:S(2)}, u32[]{:S(2)}) collective-permute-start(bf16[768,512]{1,0:T(8,128)(2,1)S(1)} %multiply_convert_fusion.13), channel_id=1, source_target_pairs={{0,2},{1,3},{2,0},{3,1},{4,6},{5,7},{6,4},{7,5},{8,10},{9,11},{10,... | collective-permute-start | bytes 2359304 | tf_op jit(solution)/shard_map/ppermute | solution.py:129
  257.0 19.6 %copy-start.20 = (bf16[1024,512]{1,0:T(8,128)(2,1)}, bf16[1024,512]{1,0:T(8,128)(2,1)S(1)}, u32[]{:S(2)}) copy-start(bf16[1024,512]{1,0:T(8,128)(2,1)S(1)} %collective-permute-done.14) | copy-start | bytes 3145732
  257.0 45.4 %collective-permute-start.21 = (bf16[1024,256]{1,0:T(8,128)(2,1)}, bf16[1024,256]{1,0:T(8,128)(2,1)}, u32[]{:S(2)}, u32[]{:S(2)}) collective-permute-start(bf16[1024,256]{1,0:T(8,128)(2,1)} %get-tuple-element.32), channel_id=1, source_target_pairs={{0,8},{8,16},{16,24},{24,0},{1,9},{9,17},{17,25},{25,1},{2,10},{10... | collective-permute-start | bytes 1572872 | tf_op jit(solution)/shard_map/ppermute | solution.py:51
  259.5 74.9 %collective-permute-start.18 = (bf16[1024,512]{1,0:T(8,128)(2,1)}, bf16[1024,512]{1,0:T(8,128)(2,1)}, u32[]{:S(2)}, u32[]{:S(2)}) collective-permute-start(bf16[1024,512]{1,0:T(8,128)(2,1)} %collective-permute-done.17), channel_id=1, source_target_pairs={{0,8},{8,16},{16,24},{24,0},{1,9},{9,17},{17,25},{25,1},{2,10},{10... | collective-permute-start | bytes 3145736 | tf_op jit(solution)/shard_map/ppermute | solution.py:51
  266.7 67.8 %collective-permute-start.11 = (bf16[1024,512]{1,0:T(8,128)(2,1)}, bf16[1024,512]{1,0:T(8,128)(2,1)}, u32[]{:S(2)}, u32[]{:S(2)}) collective-permute-start(bf16[1024,512]{1,0:T(8,128)(2,1)} %collective-permute-done.10), channel_id=1, source_target_pairs={{0,8},{8,16},{16,24},{24,0},{1,9},{9,17},{17,25},{25,1},{2,10},{10... | collective-permute-start | bytes 3145736 | tf_op jit(solution)/shard_map/ppermute | solution.py:51
  276.6 32.2 %collective-permute-start.36 = (bf16[768,512]{1,0:T(8,128)(2,1)}, bf16[768,512]{1,0:T(8,128)(2,1)}, u32[]{:S(2)}, u32[]{:S(2)}) collective-permute-start(bf16[768,512]{1,0:T(8,128)(2,1)} %multiply_convert_fusion.11), channel_id=1, source_target_pairs={{0,3},{1,2},{2,1},{3,0},{4,7},{5,6},{6,5},{7,4},{8,11},{9,10},{10,... | collective-permute-start | bytes 2359304 | tf_op jit(solution)/shard_map/ppermute | solution.py:129
  287.4 24.6 %collective-permute-start.38 = (bf16[768,512]{1,0:T(8,128)(2,1)}, bf16[768,512]{1,0:T(8,128)(2,1)}, u32[]{:S(2)}, u32[]{:S(2)}) collective-permute-start(bf16[768,512]{1,0:T(8,128)(2,1)} %multiply_convert_fusion.9), channel_id=1, source_target_pairs={{0,1},{1,0},{2,3},{3,2},{4,5},{5,4},{6,7},{7,6},{8,9},{9,8},{10,11... | collective-permute-start | bytes 2359304 | tf_op jit(solution)/shard_map/ppermute | solution.py:129
  302.4 15.3 %collective-permute-start.37 = (bf16[768,512]{1,0:T(8,128)(2,1)}, bf16[768,512]{1,0:T(8,128)(2,1)S(1)}, u32[]{:S(2)}, u32[]{:S(2)}) collective-permute-start(bf16[768,512]{1,0:T(8,128)(2,1)} %multiply_convert_fusion.10), channel_id=1, source_target_pairs={{0,2},{1,3},{2,0},{3,1},{4,6},{5,7},{6,4},{7,5},{8,10},{9,11},{10,... | collective-permute-start | bytes 2359304 | tf_op jit(solution)/shard_map/ppermute | solution.py:129
  308.8 23.6 %collective-permute-start.25 = (bf16[1024,256]{1,0:T(8,128)(2,1)S(1)}, bf16[1024,256]{1,0:T(8,128)(2,1)}, u32[]{:S(2)}, u32[]{:S(2)}) collective-permute-start(bf16[1024,256]{1,0:T(8,128)(2,1)S(1)} %copy-done.23), channel_id=1, source_target_pairs={{0,8},{8,16},{16,24},{24,0},{1,9},{9,17},{17,25},{25,1},{2,10},{10... | collective-permute-start | bytes 1572872 | tf_op jit(solution)/shard_map/ppermute | solution.py:51
  312.1 253.4 %collective-permute-start.4 = (bf16[3072,3072]{1,0:T(8,128)(2,1)S(1)}, bf16[3072,3072]{1,0:T(8,128)(2,1)}, u32[]{:S(2)}, u32[]{:S(2)}) collective-permute-start(bf16[3072,3072]{1,0:T(8,128)(2,1)S(1)} %bitcast.31), channel_id=1, source_target_pairs={{0,4},{4,0},{1,5},{5,1},{2,6},{6,2},{3,7},{7,3},{8,12},{12,8},{9,1... | collective-permute-start | bytes 56623112 | tf_op jit(solution)/shard_map/ppermute | solution.py:51
  332.5 47.5 %collective-permute-start.26 = (bf16[1024,256]{1,0:T(8,128)(2,1)}, bf16[1024,256]{1,0:T(8,128)(2,1)}, u32[]{:S(2)}, u32[]{:S(2)}) collective-permute-start(bf16[1024,256]{1,0:T(8,128)(2,1)} %collective-permute-done.25), channel_id=1, source_target_pairs={{0,8},{8,16},{16,24},{24,0},{1,9},{9,17},{17,25},{25,1},{2,10},{10... | collective-permute-start | bytes 1572872 | tf_op jit(solution)/shard_map/ppermute | solution.py:51
  334.4 39.0 %collective-permute-start.22 = (bf16[1024,256]{1,0:T(8,128)(2,1)}, bf16[1024,256]{1,0:T(8,128)(2,1)}, u32[]{:S(2)}, u32[]{:S(2)}) collective-permute-start(bf16[1024,256]{1,0:T(8,128)(2,1)} %collective-permute-done.21), channel_id=1, source_target_pairs={{0,8},{8,16},{16,24},{24,0},{1,9},{9,17},{17,25},{25,1},{2,10},{10... | collective-permute-start | bytes 1572872 | tf_op jit(solution)/shard_map/ppermute | solution.py:51
  345.2 39.4 %collective-permute-start.39 = (bf16[768,512]{1,0:T(8,128)(2,1)}, bf16[768,512]{1,0:T(8,128)(2,1)}, u32[]{:S(2)}, u32[]{:S(2)}) collective-permute-start(bf16[768,512]{1,0:T(8,128)(2,1)} %multiply_convert_fusion.8), channel_id=1, source_target_pairs={{0,3},{1,2},{2,1},{3,0},{4,7},{5,6},{6,5},{7,4},{8,11},{9,10},{10,... | collective-permute-start | bytes 2359304 | tf_op jit(solution)/shard_map/ppermute | solution.py:129
  355.8 33.2 %collective-permute-start.41 = (bf16[768,512]{1,0:T(8,128)(2,1)}, bf16[768,512]{1,0:T(8,128)(2,1)}, u32[]{:S(2)}, u32[]{:S(2)}) collective-permute-start(bf16[768,512]{1,0:T(8,128)(2,1)} %multiply_convert_fusion.6), channel_id=1, source_target_pairs={{0,1},{1,0},{2,3},{3,2},{4,5},{5,4},{6,7},{7,6},{8,9},{9,8},{10,11... | collective-permute-start | bytes 2359304 | tf_op jit(solution)/shard_map/ppermute | solution.py:129
  373.3 17.2 %collective-permute-start.40 = (bf16[768,512]{1,0:T(8,128)(2,1)}, bf16[768,512]{1,0:T(8,128)(2,1)S(1)}, u32[]{:S(2)}, u32[]{:S(2)}) collective-permute-start(bf16[768,512]{1,0:T(8,128)(2,1)} %multiply_convert_fusion.7), channel_id=1, source_target_pairs={{0,2},{1,3},{2,0},{3,1},{4,6},{5,7},{6,4},{7,5},{8,10},{9,11},{10,... | collective-permute-start | bytes 2359304 | tf_op jit(solution)/shard_map/ppermute | solution.py:129
  380.0 16.9 %collective-permute-start.23 = (bf16[1024,256]{1,0:T(8,128)(2,1)}, bf16[1024,256]{1,0:T(8,128)(2,1)S(1)}, u32[]{:S(2)}, u32[]{:S(2)}) collective-permute-start(bf16[1024,256]{1,0:T(8,128)(2,1)} %collective-permute-done.22), channel_id=1, source_target_pairs={{0,8},{8,16},{16,24},{24,0},{1,9},{9,17},{17,25},{25,1},{2,10},{10... | collective-permute-start | bytes 1572872 | tf_op jit(solution)/shard_map/ppermute | solution.py:51
  384.6 33.5 %collective-permute-start.15 = (bf16[1024,512]{1,0:T(8,128)(2,1)S(1)}, bf16[1024,512]{1,0:T(8,128)(2,1)}, u32[]{:S(2)}, u32[]{:S(2)}) collective-permute-start(bf16[1024,512]{1,0:T(8,128)(2,1)S(1)} %copy-done.21), channel_id=1, source_target_pairs={{0,8},{8,16},{16,24},{24,0},{1,9},{9,17},{17,25},{25,1},{2,10},{10... | collective-permute-start | bytes 3145736 | tf_op jit(solution)/shard_map/ppermute | solution.py:51
  418.2 57.6 %collective-permute-start.19 = (bf16[1024,512]{1,0:T(8,128)(2,1)}, bf16[1024,512]{1,0:T(8,128)(2,1)S(1)}, u32[]{:S(2)}, u32[]{:S(2)}) collective-permute-start(bf16[1024,512]{1,0:T(8,128)(2,1)} %collective-permute-done.18), channel_id=1, source_target_pairs={{0,8},{8,16},{16,24},{24,0},{1,9},{9,17},{17,25},{25,1},{2,10},{10... | collective-permute-start | bytes 3145736 | tf_op jit(solution)/shard_map/ppermute | solution.py:51
  429.9 33.5 %collective-permute-start.42 = (bf16[768,512]{1,0:T(8,128)(2,1)}, bf16[768,512]{1,0:T(8,128)(2,1)}, u32[]{:S(2)}, u32[]{:S(2)}) collective-permute-start(bf16[768,512]{1,0:T(8,128)(2,1)} %multiply_convert_fusion.5), channel_id=1, source_target_pairs={{0,3},{1,2},{2,1},{3,0},{4,7},{5,6},{6,5},{7,4},{8,11},{9,10},{10,... | collective-permute-start | bytes 2359304 | tf_op jit(solution)/shard_map/ppermute | solution.py:129
  440.5 25.1 %collective-permute-start.44 = (bf16[768,512]{1,0:T(8,128)(2,1)}, bf16[768,512]{1,0:T(8,128)(2,1)}, u32[]{:S(2)}, u32[]{:S(2)}) collective-permute-start(bf16[768,512]{1,0:T(8,128)(2,1)} %multiply_convert_fusion.3), channel_id=1, source_target_pairs={{0,1},{1,0},{2,3},{3,2},{4,5},{5,4},{6,7},{7,6},{8,9},{9,8},{10,11... | collective-permute-start | bytes 2359304 | tf_op jit(solution)/shard_map/ppermute | solution.py:129
  449.4 24.2 %collective-permute-start.43 = (bf16[768,512]{1,0:T(8,128)(2,1)}, bf16[768,512]{1,0:T(8,128)(2,1)}, u32[]{:S(2)}, u32[]{:S(2)}) collective-permute-start(bf16[768,512]{1,0:T(8,128)(2,1)} %multiply_convert_fusion.4), channel_id=1, source_target_pairs={{0,2},{1,3},{2,0},{3,1},{4,6},{5,7},{6,4},{7,5},{8,10},{9,11},{10,... | collective-permute-start | bytes 2359304 | tf_op jit(solution)/shard_map/ppermute | solution.py:129
  463.4 76.4 %collective-permute-start.48 = (bf16[768,256]{1,0:T(8,128)(2,1)}, bf16[768,256]{1,0:T(8,128)(2,1)}, u32[]{:S(2)}, u32[]{:S(2)}) collective-permute-start(bf16[768,256]{1,0:T(8,128)(2,1)} %fusion.88), channel_id=1, source_target_pairs={{0,3},{1,2},{2,1},{3,0},{4,7},{5,6},{6,5},{7,4},{8,11},{9,10},{10,... | collective-permute-start | bytes 1179656 | tf_op jit(solution)/shard_map/ppermute | solution.py:129
  475.8 35.6 %collective-permute-start.27 = (bf16[1024,256]{1,0:T(8,128)(2,1)}, bf16[1024,256]{1,0:T(8,128)(2,1)}, u32[]{:S(2)}, u32[]{:S(2)}) collective-permute-start(bf16[1024,256]{1,0:T(8,128)(2,1)} %collective-permute-done.26), channel_id=1, source_target_pairs={{0,8},{8,16},{16,24},{24,0},{1,9},{9,17},{17,25},{25,1},{2,10},{10... | collective-permute-start | bytes 1572872 | tf_op jit(solution)/shard_map/ppermute | solution.py:51
  485.2 47.2 %collective-permute-start.45 = (bf16[768,512]{1,0:T(8,128)(2,1)}, bf16[768,512]{1,0:T(8,128)(2,1)S(1)}, u32[]{:S(2)}, u32[]{:S(2)}) collective-permute-start(bf16[768,512]{1,0:T(8,128)(2,1)} %multiply_convert_fusion.2), channel_id=1, source_target_pairs={{0,3},{1,2},{2,1},{3,0},{4,7},{5,6},{6,5},{7,4},{8,11},{9,10},{10,... | collective-permute-start | bytes 2359304 | tf_op jit(solution)/shard_map/ppermute | solution.py:129
  494.3 39.4 %collective-permute-start.47 = (bf16[768,512]{1,0:T(8,128)(2,1)}, bf16[768,512]{1,0:T(8,128)(2,1)}, u32[]{:S(2)}, u32[]{:S(2)}) collective-permute-start(bf16[768,512]{1,0:T(8,128)(2,1)} %multiply_convert_fusion), channel_id=1, source_target_pairs={{0,1},{1,0},{2,3},{3,2},{4,5},{5,4},{6,7},{7,6},{8,9},{9,8},{10,11... | collective-permute-start | bytes 2359304 | tf_op jit(solution)/shard_map/ppermute | solution.py:129
  511.4 26.5 %collective-permute-start.46 = (bf16[768,512]{1,0:T(8,128)(2,1)}, bf16[768,512]{1,0:T(8,128)(2,1)}, u32[]{:S(2)}, u32[]{:S(2)}) collective-permute-start(bf16[768,512]{1,0:T(8,128)(2,1)} %multiply_convert_fusion.1), channel_id=1, source_target_pairs={{0,2},{1,3},{2,0},{3,1},{4,6},{5,7},{6,4},{7,5},{8,10},{9,11},{10,... | collective-permute-start | bytes 2359304 | tf_op jit(solution)/shard_map/ppermute | solution.py:129
  532.4 8.5 %collective-permute-start.50 = (bf16[768,256]{1,0:T(8,128)(2,1)S(1)}, bf16[768,256]{1,0:T(8,128)(2,1)S(1)}, u32[]{:S(2)}, u32[]{:S(2)}) collective-permute-start(bf16[768,256]{1,0:T(8,128)(2,1)S(1)} %copy-done.28), channel_id=1, source_target_pairs={{0,1},{1,0},{2,3},{3,2},{4,5},{5,4},{6,7},{7,6},{8,9},{9,8},{10,11... | collective-permute-start | bytes 1179656 | tf_op jit(solution)/shard_map/ppermute | solution.py:129
  533.7 8.4 %collective-permute-start.49 = (bf16[768,256]{1,0:T(8,128)(2,1)S(1)}, bf16[768,256]{1,0:T(8,128)(2,1)S(1)}, u32[]{:S(2)}, u32[]{:S(2)}) collective-permute-start(bf16[768,256]{1,0:T(8,128)(2,1)S(1)} %copy-done.27), channel_id=1, source_target_pairs={{0,2},{1,3},{2,0},{3,1},{4,6},{5,7},{6,4},{7,5},{8,10},{9,11},{10,... | collective-permute-start | bytes 1179656 | tf_op jit(solution)/shard_map/ppermute | solution.py:129
  538.0 42.6 %collective-permute-start.8 = (bf16[2048,512]{1,0:T(8,128)(2,1)S(1)}, bf16[2048,512]{1,0:T(8,128)(2,1)}, u32[]{:S(2)}, u32[]{:S(2)}) collective-permute-start(bf16[2048,512]{1,0:T(8,128)(2,1)S(1)} %copy-done.10), channel_id=1, source_target_pairs={{0,4},{4,0},{1,5},{5,1},{2,6},{6,2},{3,7},{7,3},{8,12},{12,8},{9,1... | collective-permute-start | bytes 6291464 | tf_op jit(solution)/shard_map/ppermute | solution.py:51
  539.8 13.1 %collective-permute-start.51 = (bf16[768,256]{1,0:T(8,128)(2,1)}, bf16[768,256]{1,0:T(8,128)(2,1)S(1)}, u32[]{:S(2)}, u32[]{:S(2)}) collective-permute-start(bf16[768,256]{1,0:T(8,128)(2,1)} %fusion.91), channel_id=1, source_target_pairs={{0,3},{1,2},{2,1},{3,0},{4,7},{5,6},{6,5},{7,4},{8,11},{9,10},{10,... | collective-permute-start | bytes 1179656 | tf_op jit(solution)/shard_map/ppermute | solution.py:129
  540.9 19.3 %collective-permute-start.53 = (bf16[768,256]{1,0:T(8,128)(2,1)}, bf16[768,256]{1,0:T(8,128)(2,1)S(1)}, u32[]{:S(2)}, u32[]{:S(2)}) collective-permute-start(bf16[768,256]{1,0:T(8,128)(2,1)} %fusion.93), channel_id=1, source_target_pairs={{0,1},{1,0},{2,3},{3,2},{4,5},{5,4},{6,7},{7,6},{8,9},{9,8},{10,11... | collective-permute-start | bytes 1179656 | tf_op jit(solution)/shard_map/ppermute | solution.py:129
  542.8 18.1 %collective-permute-start.52 = (bf16[768,256]{1,0:T(8,128)(2,1)}, bf16[768,256]{1,0:T(8,128)(2,1)S(1)}, u32[]{:S(2)}, u32[]{:S(2)}) collective-permute-start(bf16[768,256]{1,0:T(8,128)(2,1)} %fusion.92), channel_id=1, source_target_pairs={{0,2},{1,3},{2,0},{3,1},{4,6},{5,7},{6,4},{7,5},{8,10},{9,11},{10,... | collective-permute-start | bytes 1179656 | tf_op jit(solution)/shard_map/ppermute | solution.py:129
  552.9 113.8 %collective-permute-start.3 = (bf16[2048,512]{1,0:T(8,128)(2,1)}, bf16[2048,512]{1,0:T(8,128)(2,1)}, u32[]{:S(2)}, u32[]{:S(2)}) collective-permute-start(bf16[2048,512]{1,0:T(8,128)(2,1)} %get-tuple-element.68), channel_id=1, source_target_pairs={{0,4},{4,0},{1,5},{5,1},{2,6},{6,2},{3,7},{7,3},{8,12},{12,8},{9,1... | collective-permute-start | bytes 6291464 | tf_op jit(solution)/shard_map/ppermute | solution.py:51
  560.2 84.9 %collective-permute-start.12 = (bf16[2048,512]{1,0:T(8,128)(2,1)}, bf16[2048,512]{1,0:T(8,128)(2,1)}, u32[]{:S(2)}, u32[]{:S(2)}) collective-permute-start(bf16[2048,512]{1,0:T(8,128)(2,1)} %get-tuple-element.70), channel_id=1, source_target_pairs={{0,4},{4,0},{1,5},{5,1},{2,6},{6,2},{3,7},{7,3},{8,12},{12,8},{9,1... | collective-permute-start | bytes 6291464 | tf_op jit(solution)/shard_map/ppermute | solution.py:51
  560.9 127.8 %collective-permute-start.24 = (bf16[2048,256]{1,0:T(8,128)(2,1)}, bf16[2048,256]{1,0:T(8,128)(2,1)}, u32[]{:S(2)}, u32[]{:S(2)}) collective-permute-start(bf16[2048,256]{1,0:T(8,128)(2,1)} %get-tuple-element.78), channel_id=1, source_target_pairs={{0,4},{4,0},{1,5},{5,1},{2,6},{6,2},{3,7},{7,3},{8,12},{12,8},{9,1... | collective-permute-start | bytes 3145736 | tf_op jit(solution)/shard_map/ppermute | solution.py:51
  565.5 59.7 %collective-permute-start.16 = (bf16[2048,512]{1,0:T(8,128)(2,1)}, bf16[2048,512]{1,0:T(8,128)(2,1)}, u32[]{:S(2)}, u32[]{:S(2)}) collective-permute-start(bf16[2048,512]{1,0:T(8,128)(2,1)} %get-tuple-element.72), channel_id=1, source_target_pairs={{0,4},{4,0},{1,5},{5,1},{2,6},{6,2},{3,7},{7,3},{8,12},{12,8},{9,1... | collective-permute-start | bytes 6291464 | tf_op jit(solution)/shard_map/ppermute | solution.py:51
  580.6 21.8 %collective-permute-start.20 = (bf16[2048,512]{1,0:T(8,128)(2,1)}, bf16[2048,512]{1,0:T(8,128)(2,1)S(1)}, u32[]{:S(2)}, u32[]{:S(2)}) collective-permute-start(bf16[2048,512]{1,0:T(8,128)(2,1)} %get-tuple-element.74), channel_id=1, source_target_pairs={{0,4},{4,0},{1,5},{5,1},{2,6},{6,2},{3,7},{7,3},{8,12},{12,8},{9,1... | collective-permute-start | bytes 6291464 | tf_op jit(solution)/shard_map/ppermute | solution.py:51
  602.4 100.2 %collective-permute-start.28 = (bf16[2048,256]{1,0:T(8,128)(2,1)}, bf16[2048,256]{1,0:T(8,128)(2,1)}, u32[]{:S(2)}, u32[]{:S(2)}) collective-permute-start(bf16[2048,256]{1,0:T(8,128)(2,1)} %get-tuple-element.76), channel_id=1, source_target_pairs={{0,4},{4,0},{1,5},{5,1},{2,6},{6,2},{3,7},{7,3},{8,12},{12,8},{9,1... | collective-permute-start | bytes 3145736 | tf_op jit(solution)/shard_map/ppermute | solution.py:51
  603.7 21.6 %copy-start.9 = (bf16[3072,512]{1,0:T(8,128)(2,1)S(1)}, bf16[3072,512]{1,0:T(8,128)(2,1)}, u32[]{:S(2)}) copy-start(bf16[3072,512]{1,0:T(8,128)(2,1)} %get-tuple-element.44) | copy-start | bytes 9437188
  645.1 21.6 %copy-start.8 = (bf16[3072,512]{1,0:T(8,128)(2,1)S(1)}, bf16[3072,512]{1,0:T(8,128)(2,1)}, u32[]{:S(2)}) copy-start(bf16[3072,512]{1,0:T(8,128)(2,1)} %get-tuple-element.46) | copy-start | bytes 9437188
  (28 other events, 268.4 us)

commit v2 on v0

v2 whole, which is shorter than its diff:
```python
import functools

import jax
import jax.numpy as jnp
from jax import lax
from jax.experimental import pallas as pl
from jax.experimental.pallas import tpu as pltpu
from jax.sharding import PartitionSpec as P

SQRT_TWO_PI = 0.7978845608028654
CUBIC = 0.044715
VMEM_LIMIT = 56 * 1024 * 1024
BLOCK = 768
SHARES = 24
STAGES = ((10, 0), (8, 16), (4, 12), (2, 10))

ANY = pl.BlockSpec(memory_space=pl.ANY)
TOKEN = jax.ShapeDtypeStruct((8, 128), jnp.float32)
FREE = pl.CostEstimate(flops=0, bytes_accessed=0, transcendentals=0)


def gelu_pair(x):
    square = x * x
    bent = jnp.tanh(x * (SQRT_TWO_PI + (SQRT_TWO_PI * CUBIC) * square))
    rise = x * (SQRT_TWO_PI + (3.0 * SQRT_TWO_PI * CUBIC) * square)
    up = 0.5 + 0.5 * bent
    return x * up, up + rise * (0.5 - 0.5 * (bent * bent))


def params():
    return pltpu.CompilerParams(vmem_limit_bytes=VMEM_LIMIT)


def divisor(size, most, unit):
    for block in range(most - most % unit, 0, -unit):
        if size % block == 0:
            return block
    return size


def stages_of(width):
    if width % (SHARES * 128) == 0:
        share = width // SHARES
        return [(w * share, at * share) for w, at in STAGES]
    return [(width, 0)]


def swap(x, axis, size, step):
    return lax.ppermute(x, axis, [(i, (i + step) % size) for i in range(size)])


def cut(token, array, width, first):
    rows = array.shape[0]
    tall = divisor(rows, 256, 16)

    def kernel(array_ref, token_ref, out_ref, token_out):
        out_ref[...] = array_ref[...]

    out = pl.pallas_call(
        kernel,
        out_shape=[jax.ShapeDtypeStruct((rows, width), array.dtype), TOKEN],
        grid=(rows // tall,),
        in_specs=[pl.BlockSpec((tall, width), lambda i: (i, first // width)), ANY],
        out_specs=[pl.BlockSpec((tall, width), lambda i: (i, 0)), ANY],
        cost_estimate=FREE,
        compiler_params=params(),
    )(array, token)
    return out[1], out[0]


def activate(token, pre_act):
    rows, hidden = pre_act.shape
    tall, wide = divisor(rows, 512, 128), divisor(hidden, 512, 128)

    def kernel(x_ref, token_ref, out_ref, slopes_ref, token_out):
        value, slopes = gelu_pair(x_ref[...].astype(jnp.float32))
        out_ref[...] = value.T.astype(jnp.bfloat16)
        slopes_ref[...] = slopes

    tile = pl.BlockSpec((tall, wide), lambda j, i: (i, j))
    out = pl.pallas_call(
        kernel,
        out_shape=[
            jax.ShapeDtypeStruct((hidden, rows), jnp.bfloat16),
            jax.ShapeDtypeStruct((rows, hidden), jnp.float32),
            TOKEN,
        ],
        grid=(hidden // wide, rows // tall),
        in_specs=[tile, ANY],
        out_specs=[pl.BlockSpec((wide, tall), lambda j, i: (j, i)), tile, ANY],
        cost_estimate=FREE,
        compiler_params=params(),
    )(pre_act, token)
    return out[2], out[0], out[1]


def terms(token, table, pieces, acts, part, group, send, factor, with_rows):
    nc, rows, width = len(acts), acts[0].shape[1], pieces[0][0].shape[1]
    hidden = acts[0].shape[0]
    block = divisor(part, BLOCK if width <= 1024 else BLOCK // 2, 16)
    blocks = part // block
    base = len(pieces)
    steps = len(group) * blocks
    away = (len(group) - group.count(0)) * blocks
    own = group[-1] == 0
    strip = rows // steps if with_rows else 0

    def kernel(table_ref, *refs):
        refs = list(refs)
        piece_refs = [refs.pop(0) for _ in pieces]
        act_refs = [refs.pop(0) for _ in acts]
        refs.pop(0)
        if send is not None:
            refs.pop(0)
        send_ref = refs.pop(0) if away else None
        own_ref = refs.pop(0) if own else None
        row_outs = [refs.pop(0) for _ in range(nc if with_rows else 0)]
        refs.pop(0)
        held, sems = refs
        i = pl.program_id(0)

        @pl.when(i == 0)
        def _():
            copies = []
            for p, (_, first, count, place) in enumerate(pieces):
                to = pl.multiple_of(table_ref[place], 16)
                copies.append(
                    pltpu.make_async_copy(
                        piece_refs[p].at[pl.ds(first, count)], held.at[pl.ds(to, count)], sems.at[p]
                    )
                )
            for copy in copies:
                copy.start()
            for copy in copies:
                copy.wait()

        for j, ref in enumerate(row_outs):
            ref[...] = held[pl.ds(pl.multiple_of(j * rows + i * strip, 16), strip), :]
        total = None
        for j in range(nc):
            term = jnp.dot(
                act_refs[j][...],
                held[j * rows : (j + 1) * rows, :],
                preferred_element_type=jnp.float32,
            )
            total = term if total is None else total + term
        total = total * factor
        if away and own:

            @pl.when(i < away)
            def _():
                send_ref[...] = total.astype(send_ref.dtype)

            @pl.when(i >= away)
            def _():
                own_ref[...] = total

        elif own:
            own_ref[...] = total
        else:
            send_ref[...] = total.astype(send_ref.dtype)

    def act_map(i, table_ref):
        distance = group[0] - i // blocks
        return table_ref[base + distance] * blocks + i % blocks, 0

    def send_map(i, table_ref):
        return act_map(jnp.minimum(i, away - 1), table_ref)

    shapes, specs, aliases = [], [], {}
    operands = [p[0] for p in pieces] + list(acts) + [token]
    in_specs = [ANY] * len(pieces) + [pl.BlockSpec((block, rows), act_map)] * nc + [ANY]
    if send is not None:
        operands.append(send)
        in_specs.append(ANY)
        if away:
            aliases = {len(operands): 0}
    if away:
        shapes.append(jax.ShapeDtypeStruct((hidden, width), jnp.bfloat16))
        specs.append(pl.BlockSpec((block, width), send_map))
    if own:
        shapes.append(jax.ShapeDtypeStruct((part, width), jnp.float32))
        specs.append(
            pl.BlockSpec((block, width), lambda i, t: (jnp.clip(i - away, 0, blocks - 1), 0))
        )
    if with_rows:
        shapes += [jax.ShapeDtypeStruct((rows, width), jnp.bfloat16)] * nc
        specs += [pl.BlockSpec((strip, width), lambda i, t: (i, 0))] * nc
    out = list(
        pl.pallas_call(
            kernel,
            out_shape=shapes + [TOKEN],
            grid_spec=pltpu.PrefetchScalarGridSpec(
                num_scalar_prefetch=1,
                grid=(steps,),
                in_specs=in_specs,
                out_specs=specs + [ANY],
                scratch_shapes=[
                    pltpu.VMEM((nc * rows, width), jnp.bfloat16),
                    pltpu.SemaphoreType.DMA((len(pieces),)),
                ],
            ),
            input_output_aliases=aliases,
            cost_estimate=FREE,
            compiler_params=params(),
        )(table, *operands)
    )
    sent = out.pop(0) if away else send
    kept = out.pop(0) if own else None
    return out[-1], sent, kept, out[:-1]


def products(token, features, weights, span, total, slopes):
    width, first = span
    rows, hidden = features[0].shape[0], weights[0].shape[0]
    nc = len(weights)
    last = slopes is not None
    tall = divisor(rows, 512 if nc * width <= 1024 else 256, 16)

    def kernel(*refs):
        refs = list(refs)
        lefts = [refs.pop(0) for _ in range(nc)]
        rights = [refs.pop(0) for _ in range(nc)]
        total_ref = refs.pop(0) if total is not None else None
        slopes_ref = refs.pop(0) if last else None
        out_ref = refs[1]
        value = None
        for left, right in zip(lefts, rights):
            term = lax.dot_general(
                left[...],
                right[...],
                (((1,), (1,)), ((), ())),
                preferred_element_type=jnp.float32,
            )
            value = term if value is None else value + term
        if total_ref is not None:
            value = value + total_ref[...]
        if last:
            value = value * slopes_ref[...]
        out_ref[...] = value.astype(out_ref.dtype)

    tile = pl.BlockSpec((tall, hidden), lambda i: (i, 0))
    operands = list(features) + list(weights)
    specs = [pl.BlockSpec((tall, width), lambda i: (i, 0))] * nc
    specs += [
        pl.BlockSpec(
            (hidden, width), lambda i: (0, first // width), pipeline_mode=pl.Buffered(1)
        )
    ] * nc
    aliases = {}
    if total is not None:
        if not last:
            aliases = {len(operands): 0}
        operands.append(total)
        specs.append(tile)
    if last:
        operands.append(slopes)
        specs.append(tile)
    kind = jnp.bfloat16 if last else jnp.float32
    out = pl.pallas_call(
        kernel,
        out_shape=[jax.ShapeDtypeStruct((rows, hidden), kind), TOKEN],
        grid=(rows // tall,),
        in_specs=specs + [ANY],
        out_specs=[tile, ANY],
        input_output_aliases=aliases,
        cost_estimate=FREE,
        compiler_params=params(),
    )(*operands, token)
    return out[1], out[0]


def add_up(token, table, base, own, arrived, whole, shape, span):
    width, first = span
    rows = shape[0]
    tall = divisor(rows, 384, 16)
    steps = rows // tall
    count = arrived.shape[0] // rows - 1

    def kernel(table_ref, *refs):
        value = refs[0][...]
        for ref in refs[1 : 1 + count]:
            value = value + ref[...].astype(jnp.float32)
        refs[-2][...] = value

    def other(d):
        return pl.BlockSpec((tall, width), lambda i, t: (t[base + d] * steps + i, 0))

    operands = [own] + [arrived] * count
    specs, aliases = [pl.BlockSpec((tall, width), lambda i, t: (i, 0))], {}
    specs += [other(d) for d in range(1, count + 1)]
    if whole is not None:
        aliases = {len(operands) + 1: 0}
        operands.append(whole)
        specs.append(ANY)
    out = pl.pallas_call(
        kernel,
        out_shape=[jax.ShapeDtypeStruct(shape, jnp.float32), TOKEN],
        grid_spec=pltpu.PrefetchScalarGridSpec(
            num_scalar_prefetch=1,
            grid=(steps,),
            in_specs=specs + [ANY],
            out_specs=[pl.BlockSpec((tall, width), lambda i, t: (i, first // width)), ANY],
        ),
        input_output_aliases=aliases,
        cost_estimate=FREE,
        compiler_params=params(),
    )(table, *operands, token)
    return out[1], out[0]


def on_device(n, nc, nr, pre_act, w_out, grad_out):
    tokens = grad_out.shape[0] * n * nr
    factor = float(tokens) ** (-0.5)
    col, rep = lax.axis_index("col"), lax.axis_index("rep")
    rows, hidden = pre_act.shape
    part = hidden // nr
    shape = (part, grad_out.shape[1])
    spans = stages_of(grad_out.shape[1])
    count = len(spans)
    distances = list(range(nr - 1, -1, -1))

    def partner(d):
        return rep ^ d if nr & (nr - 1) == 0 else (rep + d) % nr

    places = [((j - col + nc) % nc) * rows for j in range(nc)]
    table = jnp.stack([jnp.int32(v) for v in places + [partner(d) for d in range(nr)]])
    token = jnp.zeros(TOKEN.shape, TOKEN.dtype)
    gathered, features, owns, arrived = {}, {}, {}, {}
    grad_act = grad_weight = None

    def gather(token, k):
        if k >= count:
            return token
        token, columns = cut(token, grad_out, *spans[k])
        gathered[k] = lax.all_gather(columns, "row", axis=0, tiled=True)
        return token

    token = gather(token, 0)
    token = gather(token, 1)
    token, act, slopes = activate(token, pre_act)
    acts = [act] + [swap(act, "col", nc, nc - j) for j in range(1, nc)]
    weights = [w_out] + [swap(w_out, "col", nc, nc - j) for j in range(1, nc)]
    token = gather(token, 2)

    for k in range(count):
        listed = [(gathered[k], j * rows, rows, j) for j in range(nc)]
        token, sent, own, own_rows = terms(
            token, table, listed, acts, part, distances, None, factor, True
        )
        features[k] = [own_rows[0]] + [swap(own_rows[j], "col", nc, j) for j in range(1, nc)]
        owns[k] = arrived[k] = own
        if nr > 1:
            arrived[k] = lax.all_to_all(sent, "rep", 0, 0, tiled=True)
        token = gather(token, k + 3)
        if k > 0:
            token, grad_weight = add_up(
                token, table, nc, owns[k - 1], arrived[k - 1], grad_weight, shape, spans[k - 1]
            )
        token, grad_act = products(
            token, features[k], weights, spans[k], grad_act, slopes if k == count - 1 else None
        )
    token, grad_weight = add_up(
        token, table, nc, owns[count - 1], arrived[count - 1], grad_weight, shape, spans[count - 1]
    )
    return grad_act, grad_weight


def solution(mesh):
    n, nc, nr = (mesh.shape[axis] for axis in ("row", "col", "rep"))
    in_specs = (P(("rep", "col"), "row"), P("row", "col"), P(("rep", "row"), "col"))
    out_specs = (P(("rep", "col"), "row"), P(("row", "rep"), "col"))
    return jax.shard_map(
        functools.partial(on_device, n, nc, nr),
        mesh=mesh,
        in_specs=in_specs,
        out_specs=out_specs,
        check_vma=False,
    )
```

time: 1080 us -> 560 us (0.52)
  waiting for transfers between devices: 857 us -> 208 us
  Pallas kernels: 0 us -> 313 us
  matrix products: 178 us -> 0 us
  other arithmetic: 27.2 us -> 0 us
  starting transfers between devices: 0.16 us -> 20.7 us
    reduce_scatter x1 -> x0, waiting for transfers between devices: 324 us -> none  [on_device(): lax.psum_scatter(whole * factor, 'rep', scatter_dimension=0, tiled=True)]
    pallas_call x0 -> x17, Pallas kernels: none -> 313 us  [the longest x4 127 us: products(): pl.pallas_call(kernel, out_shape=[jax.ShapeDtypeStruct((rows, hidden), ki...]
    all_gather x2 -> x4, waiting for transfers between devices: 471 us -> 182 us  [gather(): gathered[k] = lax.all_gather(columns, 'row', axis=0, tiled=True)]
    dot_general x2 -> x0, matrix products: 178 us -> none  [the longest x1 89.7 us: contract_rows(): lax.dot_general(left, right, (((0,), (0,)), ((), ())), preferred_element_...]
    unnamed x5 -> x4, waiting for transfers between devices: 62.4 us -> 0.67 us
    convert_element_type x1 -> x0, other arithmetic: 27.2 us -> none  [on_device(): activation = output.astype(jnp.bfloat16)]
    ppermute x0 -> x6, waiting for transfers between devices: none -> 21.5 us  [swap(): return lax.ppermute(x, axis, [(i, (i + step) % size) for i in range(size)])]
    all_to_all x0 -> x4, starting transfers between devices: none -> 18.9 us  [on_device(): arrived[k] = lax.all_to_all(sent, 'rep', 0, 0, tiled=True)]
  transfers between devices with their start and end apart: 4 -> 14, of which waited for: 4 -> 6; matrix products, arithmetic and copies ran while one was open for 0% -> 0% of each run, Pallas kernels for 0% -> 55%
where the time goes in v2:
time: 560 us; the launch traced here: 559 us
  Pallas kernels  313 us (56%)
  waiting for transfers between devices  208 us (37%)
  starting transfers between devices  20.7 us (4%)
  between operations  13.9 us (2%)
    all_gather x4, waiting for transfers between devices, gather(): gathered[k] = lax.all_gather(columns, 'row', axis=0, tiled=True)  182 us
    pallas_call x4, Pallas kernels, products(): pl.pallas_call(kernel, out_shape=[jax.ShapeDtypeStruct((rows, hidden), ki...  127 us
    pallas_call x4, Pallas kernels, terms(): pl.pallas_call(kernel, out_shape=shapes + [TOKEN], grid_spec=pltpu.Prefet...  124 us
    pallas_call x1, Pallas kernels, activate(): pl.pallas_call(kernel, out_shape=[jax.ShapeDtypeStruct((hidden, rows), jn...  28.3 us
    ppermute x6, waiting for transfers between devices, swap(): return lax.ppermute(x, axis, [(i, (i + step) % size) for i in range(size)])  21.5 us
    all_to_all x4, starting transfers between devices, on_device(): arrived[k] = lax.all_to_all(sent, 'rep', 0, 0, tiled=True)  18.9 us
    pallas_call x4, Pallas kernels, add_up(): pl.pallas_call(kernel, out_shape=[jax.ShapeDtypeStruct(shape, jnp.float32...  18.8 us
    pallas_call x4, Pallas kernels, cut(): pl.pallas_call(kernel, out_shape=[jax.ShapeDtypeStruct((rows, width), arr...  14.3 us
  transfers between devices with their start and end apart: 14, of which 6 were waited for; matrix products, arithmetic and copies ran while one was open for 0% of the time, Pallas kernels for 55%

profile of v2, /device:TPU:0, one launch (start us, length us, event | category | flops | bytes accessed | tf_op | source)
XLA Modules:
  0.0 558.8 jit_solution(13280018012474614949)
XLA Ops:
  7.2 0.0 all-gather.5.cloned.1.call-start
  7.2 0.6 broadcast_in_dim.3.token_ref
  7.8 4.0 shard_map.50
  11.8 0.0 all-gather.5.cloned.1.call-update
  11.8 0.0 all-gather.11.cloned.1.call-start
  11.9 0.5 collective-permute-start.2
  12.4 3.8 shard_map.51
  16.2 28.3 %shard_map.52 = (bf16[3072,2048]{1,0:T(8,128)(2,1)}, f32[2048,3072]{1,0:T(8,128)}, f32[8,128]{1,0:T(8,128)}) custom-call(bf16[2048,3072]{1,0:T(8,128)(2,1)} %x_ref.1, f32[8,128]{1,0:T(8,128)} %get-tuple-element.50.token_ref), custom_call_target="tpu_custom_call" | custom-call | tf_op jit(solution)/shard_map/pallas_call | solution.py:81
  44.5 0.0 collective-permute-start
  44.5 0.0 all-gather.11.cloned.1.call-update
  44.5 3.4 shard_map.53
  47.9 0.7 stack.27.table_ref
  48.5 15.4 %collective-permute-done.refs_3_ = bf16[3072,2048]{1,0:T(8,128)(2,1)} collective-permute-done((bf16[3072,2048]{1,0:T(8,128)(2,1)}, bf16[3072,2048]{1,0:T(8,128)(2,1)}, u32[]{:S(2)}, u32[]{:S(2)}) %collective-permute-start) | collective-permute-done | bytes 12582944 | tf_op jit(solution)/shard_map/ppermute | solution.py:49
  64.0 134.6 %all-gather.5.cloned.1.call-done.refs_0_.refs_1_ = bf16[4096,1280]{1,0:T(8,128)(2,1)} async-done(((bf16[1024,1280]{1,0:T(8,128)(2,1)}), bf16[4096,1280]{1,0:T(8,128)(2,1)}) %all-gather.5.cloned.1.call-update) | async-done | bytes 10485776 | tf_op jit(solution)/shard_map/all_gather | solution.py:336
  198.6 45.3 %shard_map.54 = (bf16[3072,1280]{1,0:T(8,128)(2,1)}, f32[768,1280]{1,0:T(8,128)}, bf16[2048,1280]{1,0:T(8,128)(2,1)}, bf16[2048,1280]{1,0:T(8,128)(2,1)}, f32[8,128]{1,0:T(8,128)}) custom-call(s32[6]{0:T(128)} %stack.27.table_ref, bf16[4096,1280]{1,0:T(8,128)(2,1)} %all-gather.5.cloned.1.call-done.refs_0_.refs_1_, ...), custom_call_target="tpu_custom_call" | custom-call | tf_op jit(solution)/shard_map/pallas_call | solution.py:190
  243.9 5.6 all-to-all-start
  249.4 0.2 all-gather.9.cloned.1.call-start
  249.7 0.1 collective-permute-start.1
  249.8 0.4 all-gather.9.cloned.1.call-update
  250.2 3.1 shard_map.55
  253.3 0.0 collective-permute-done.2.refs_3_
  253.3 5.4 collective-permute-done.1.refs_1_
  258.7 41.9 %shard_map.56 = (f32[2048,3072]{1,0:T(8,128)}, f32[8,128]{1,0:T(8,128)}) custom-call(bf16[2048,1280]{1,0:T(8,128)(2,1)} %get-tuple-element.58.refs_0_, bf16[2048,1280]{1,0:T(8,128)(2,1)} %collective-permute-done.1.refs_1_, bf16[3072,3072]{1,0:T(8,128)(2,1)} %refs_2_.7, bf16[3072,3072]{1,0:T(8,128)(2,1)} %collective-permute-done.2.refs_3_, ...), custom_call_target="tpu_custom_call" | custom-call | tf_op jit(solution)/shard_map/pallas_call | solution.py:260
  300.6 47.4 %all-gather.11.cloned.1.call-done.refs_0_.refs_1_ = bf16[4096,1024]{1,0:T(8,128)(2,1)} async-done(((bf16[1024,1024]{1,0:T(8,128)(2,1)}), bf16[4096,1024]{1,0:T(8,128)(2,1)}) %all-gather.11.cloned.1.call-update) | async-done | bytes 8388624 | tf_op jit(solution)/shard_map/all_gather | solution.py:336
  348.0 39.4 %shard_map.57 = (bf16[3072,1024]{1,0:T(8,128)(2,1)}, f32[768,1024]{1,0:T(8,128)}, bf16[2048,1024]{1,0:T(8,128)(2,1)}, bf16[2048,1024]{1,0:T(8,128)(2,1)}, f32[8,128]{1,0:T(8,128)}) custom-call(s32[6]{0:T(128)} %stack.27.table_ref, bf16[4096,1024]{1,0:T(8,128)(2,1)} %all-gather.11.cloned.1.call-done.refs_0_.refs_1_, ...), custom_call_target="tpu_custom_call" | custom-call | tf_op jit(solution)/shard_map/pallas_call | solution.py:190
  387.4 0.0 all-to-all-done
  387.4 5.3 all-to-all-start.1
  392.7 0.3 all-gather.7.cloned.1.call-start
  393.0 0.1 collective-permute-start.3
  393.0 0.2 all-gather.7.cloned.1.call-update
  393.3 6.6 %shard_map.58 = (f32[768,3072]{1,0:T(8,128)}, f32[8,128]{1,0:T(8,128)}) custom-call(s32[6]{0:T(128)} %stack.27.table_ref, f32[768,1280]{1,0:T(8,128)} %get-tuple-element.65.refs_0_, bf16[3072,1280]{1,0:T(8,128)(2,1)} %bitcast.7.refs_1_.refs_2_.refs_3_, bf16[3072,1280]{1,0:T(8,128)(2,1)} %bitcast.7.refs_1_.refs_2_.refs_3_, ...), custom_call_target="tpu_custom_call" | custom-call | tf_op jit(solution)/shard_map/pallas_call | solution.py:296
  399.9 0.7 collective-permute-done.3.refs_1_
  400.5 35.7 %shard_map.59 = (f32[2048,3072]{1,0:T(8,128)}, f32[8,128]{1,0:T(8,128)}) custom-call(bf16[2048,1024]{1,0:T(8,128)(2,1)} %get-tuple-element.62.refs_0_, bf16[2048,1024]{1,0:T(8,128)(2,1)} %collective-permute-done.3.refs_1_, bf16[3072,3072]{1,0:T(8,128)(2,1)} %refs_2_.7, ...), custom_call_target="tpu_custom_call", output_to_operand_aliasing={{0}: (4, {})} | custom-call | tf_op jit(solution)/shard_map/pallas_call | solution.py:260
  436.2 0.0 all-gather.9.cloned.1.call-done.refs_0_.refs_1_
  436.2 23.1 %shard_map.60 = (bf16[3072,512]{1,0:T(8,128)(2,1)}, f32[768,512]{1,0:T(8,128)}, bf16[2048,512]{1,0:T(8,128)(2,1)}, bf16[2048,512]{1,0:T(8,128)(2,1)}, f32[8,128]{1,0:T(8,128)}) custom-call(s32[6]{0:T(128)} %stack.27.table_ref, bf16[4096,512]{1,0:T(8,128)(2,1)} %all-gather.9.cloned.1.call-done.refs_0_.refs_1_, ...), custom_call_target="tpu_custom_call" | custom-call | tf_op jit(solution)/shard_map/pallas_call | solution.py:190
  459.3 3.7 all-to-all-done.1
  463.0 3.7 all-to-all-start.2
  466.7 0.1 collective-permute-start.4
  466.8 5.4 shard_map.61
  472.1 0.0 collective-permute-done.4.refs_1_
  472.1 0.0 copy-start.1
  472.1 1.3 copy-done.1
  473.5 25.7 %shard_map.62 = (f32[2048,3072]{1,0:T(8,128)}, f32[8,128]{1,0:T(8,128)}) custom-call(bf16[2048,512]{1,0:T(8,128)(2,1)} %get-tuple-element.70.refs_0_, bf16[2048,512]{1,0:T(8,128)(2,1)} %copy-done.1, bf16[3072,3072]{1,0:T(8,128)(2,1)} %refs_2_.7, bf16[3072,3072]{1,0:T(8,128)(2,1)} %collective-permute-done.2.refs_3_, ...), custom_call_target="tpu_custom_call", output_to_operand_aliasing={{0}: (4, {})} | custom-call | tf_op jit(solution)/shard_map/pallas_call | solution.py:260
  499.2 0.0 all-gather.7.cloned.1.call-done.refs_0_.refs_1_
  499.2 16.5 %shard_map.63 = (bf16[3072,256]{1,0:T(8,128)(2,1)}, f32[768,256]{1,0:T(8,128)}, bf16[2048,256]{1,0:T(8,128)(2,1)}, bf16[2048,256]{1,0:T(8,128)(2,1)}, f32[8,128]{1,0:T(8,128)}) custom-call(s32[6]{0:T(128)} %stack.27.table_ref, bf16[4096,256]{1,0:T(8,128)(2,1)} %all-gather.7.cloned.1.call-done.refs_0_.refs_1_, ...), custom_call_target="tpu_custom_call" | custom-call | tf_op jit(solution)/shard_map/pallas_call | solution.py:190
  515.7 0.0 all-to-all-done.2
  515.7 0.0 copy-start
  515.7 4.4 all-to-all-start.3
  520.1 0.5 collective-permute-start.5
  520.6 0.0 copy-done
  520.6 3.8 shard_map.64
  524.4 0.0 collective-permute-done.5.refs_1_
  524.4 0.0 copy-start.2
  524.4 1.0 copy-done.2
  525.4 23.8 %shard_map.65 = (bf16[2048,3072]{1,0:T(8,128)(2,1)}, f32[8,128]{1,0:T(8,128)}) custom-call(bf16[2048,256]{1,0:T(8,128)(2,1)} %get-tuple-element.79.refs_0_, bf16[2048,256]{1,0:T(8,128)(2,1)} %copy-done.2, bf16[3072,3072]{1,0:T(8,128)(2,1)} %refs_2_.7, bf16[3072,3072]{1,0:T(8,128)(2,1)} %collective-permute-done.2.refs_3_, ...), custom_call_target="tpu_custom_call" | custom-call | tf_op jit(solution)/shard_map/pallas_call | solution.py:260
  549.3 0.0 all-to-all-done.3
  549.3 3.0 shard_map.66
Async XLA Ops:
  7.2 191.4 %all-gather.5.cloned.1.call-start = ((), (), s32[]{:S(2)}) async-start(), calls=%async_computation.4 | async-start | bytes 13107200 | tf_op jit(solution)/shard_map/all_gather | solution.py:336
  11.8 336.2 %all-gather.11.cloned.1.call-start = ((), (), s32[]{:S(2)}) async-start(), calls=%async_computation.7 | async-start | bytes 10485760 | tf_op jit(solution)/shard_map/all_gather | solution.py:336
  11.9 241.5 %collective-permute-start.2 = (bf16[3072,3072]{1,0:T(8,128)(2,1)}, bf16[3072,3072]{1,0:T(8,128)(2,1)}, u32[]{:S(2)}, u32[]{:S(2)}) collective-permute-start(bf16[3072,3072]{1,0:T(8,128)(2,1)} %refs_2_.7), channel_id=1, source_target_pairs={{0,4},{4,0},{1,5},{5,1},{2,6},{6,2},{3,7},{7,3},{8,12},{12,8},{9,1... | collective-permute-start | bytes 56623112 | tf_op jit(solution)/shard_map/ppermute | solution.py:49
  44.5 19.5 %collective-permute-start = (bf16[3072,2048]{1,0:T(8,128)(2,1)}, bf16[3072,2048]{1,0:T(8,128)(2,1)}, u32[]{:S(2)}, u32[]{:S(2)}) collective-permute-start(bf16[3072,2048]{1,0:T(8,128)(2,1)} %get-tuple-element.51.refs_2_), channel_id=1, source_target_pairs={{0,4},{4,0},{1,5},{5,1},{2,6},{6,2},{3,7},{7,3},{8,12},{12,8},{9,1... | collective-permute-start | bytes 37748744 | tf_op jit(solution)/shard_map/ppermute | solution.py:49
  243.9 143.5 %all-to-all-start = ((bf16[4,768,1280]{2,1,0:T(8,128)(2,1)}), bf16[4,768,1280]{2,1,0:T(8,128)(2,1)}, u32[]{:S(2)}, u32[]{:S(2)}) async-start(bf16[4,768,1280]{2,1,0:T(8,128)(2,1)} %bitcast.17), calls=%async_computation | async-start | bytes 15728640 | tf_op jit(solution)/shard_map/all_to_all | solution.py:354
  249.4 186.7 %all-gather.9.cloned.1.call-start = ((), (), s32[]{:S(2)}) async-start(), calls=%async_computation.6 | async-start | bytes 5242880 | tf_op jit(solution)/shard_map/all_gather | solution.py:336
  249.7 9.1 %collective-permute-start.1 = (bf16[2048,1280]{1,0:T(8,128)(2,1)}, bf16[2048,1280]{1,0:T(8,128)(2,1)}, u32[]{:S(2)}, u32[]{:S(2)}) collective-permute-start(bf16[2048,1280]{1,0:T(8,128)(2,1)} %get-tuple-element.59), channel_id=1, source_target_pairs={{0,4},{4,0},{1,5},{5,1},{2,6},{6,2},{3,7},{7,3},{8,12},{12,8},{9,1... | collective-permute-start | bytes 15728648 | tf_op jit(solution)/shard_map/ppermute | solution.py:49
  387.4 75.5 %all-to-all-start.1 = ((bf16[4,768,1024]{2,1,0:T(8,128)(2,1)}), bf16[4,768,1024]{2,1,0:T(8,128)(2,1)}, u32[]{:S(2)}, u32[]{:S(2)}) async-start(bf16[4,768,1024]{2,1,0:T(8,128)(2,1)} %bitcast.18), calls=%async_computation.1 | async-start | bytes 12582912 | tf_op jit(solution)/shard_map/all_to_all | solution.py:354
  392.7 106.5 %all-gather.7.cloned.1.call-start = ((), (), s32[]{:S(2)}) async-start(), calls=%async_computation.5 | async-start | bytes 2621440 | tf_op jit(solution)/shard_map/all_gather | solution.py:336
  393.0 7.6 %collective-permute-start.3 = (bf16[2048,1024]{1,0:T(8,128)(2,1)}, bf16[2048,1024]{1,0:T(8,128)(2,1)}, u32[]{:S(2)}, u32[]{:S(2)}) collective-permute-start(bf16[2048,1024]{1,0:T(8,128)(2,1)} %get-tuple-element.63), channel_id=1, source_target_pairs={{0,4},{4,0},{1,5},{5,1},{2,6},{6,2},{3,7},{7,3},{8,12},{12,8},{9,1... | collective-permute-start | bytes 12582920 | tf_op jit(solution)/shard_map/ppermute | solution.py:49
  463.0 52.7 %all-to-all-start.2 = ((bf16[4,768,512]{2,1,0:T(8,128)(2,1)}), bf16[4,768,512]{2,1,0:T(8,128)(2,1)S(1)}, u32[]{:S(2)}, u32[]{:S(2)}) async-start(bf16[4,768,512]{2,1,0:T(8,128)(2,1)} %bitcast.19), calls=%async_computation.2 | async-start | bytes 6291456 | tf_op jit(solution)/shard_map/all_to_all | solution.py:354
  466.7 5.5 collective-permute-start.4
  472.1 1.3 copy-start.1
  515.7 4.9 copy-start
  515.7 33.6 %all-to-all-start.3 = ((bf16[4,768,256]{2,1,0:T(8,128)(2,1)}), bf16[4,768,256]{2,1,0:T(8,128)(2,1)}, u32[]{:S(2)}, u32[]{:S(2)}) async-start(bf16[4,768,256]{2,1,0:T(8,128)(2,1)} %bitcast.20), calls=%async_computation.3 | async-start | bytes 3145728 | tf_op jit(solution)/shard_map/all_to_all | solution.py:354
  520.1 4.3 collective-permute-start.5
  524.4 1.0 copy-start.2
Sparse Core Ops, SparseCore 0:
  11.9 186.6 all-gather.4
  200.2 147.8 all-gather.10
  349.6 78.9 all-gather.8
  430.0 44.4 all-gather.6

commit v3 on v2

--- a/solution.py
+++ b/solution.py
@@ -12,7 +12,10 @@
 VMEM_LIMIT = 56 * 1024 * 1024
 BLOCK = 768
 SHARES = 24
-STAGES = ((10, 0), (8, 16), (4, 12), (2, 10))
+STAGES = ((2, 10), (10, 0), (8, 16), (4, 12))
+RING_LIMIT = 8
+PERMUTED, LATE = 1, 1
+GROUPS = ((0,), (1,), (2,), (3,))
 
 ANY = pl.BlockSpec(memory_space=pl.ANY)
 TOKEN = jax.ShapeDtypeStruct((8, 128), jnp.float32)
@@ -47,6 +50,22 @@
 
 def swap(x, axis, size, step):
     return lax.ppermute(x, axis, [(i, (i + step) % size) for i in range(size)])
+
+
+def pass_on(token, array):
+    def kernel(*refs):
+        pass
+
+    out = pl.pallas_call(
+        kernel,
+        out_shape=[jax.ShapeDtypeStruct(array.shape, array.dtype), TOKEN],
+        in_specs=[ANY] * 2,
+        out_specs=[ANY] * 2,
+        input_output_aliases={0: 0},
+        cost_estimate=FREE,
+        compiler_params=params(),
+    )(array, token)
+    return out[1], out[0]
 
 
 def cut(token, array, width, first):
@@ -94,12 +113,11 @@
     return out[2], out[0], out[1]
 
 
-def terms(token, table, pieces, acts, part, group, send, factor, with_rows):
+def terms(token, table, base, pieces, acts, part, group, send, factor, with_rows):
     nc, rows, width = len(acts), acts[0].shape[1], pieces[0][0].shape[1]
     hidden = acts[0].shape[0]
     block = divisor(part, BLOCK if width <= 1024 else BLOCK // 2, 16)
     blocks = part // block
-    base = len(pieces)
     steps = len(group) * blocks
     away = (len(group) - group.count(0)) * blocks
     own = group[-1] == 0
@@ -210,17 +228,17 @@
     return out[-1], sent, kept, out[:-1]
 
 
-def products(token, features, weights, span, total, slopes):
-    width, first = span
-    rows, hidden = features[0].shape[0], weights[0].shape[0]
+def products(token, features, weights, spans, total, slopes):
+    rows, hidden = features[0][0].shape[0], weights[0].shape[0]
     nc = len(weights)
     last = slopes is not None
-    tall = divisor(rows, 512 if nc * width <= 1024 else 256, 16)
+    wide = nc * sum(width for width, _ in spans)
+    tall = divisor(rows, 512 if wide <= 1024 else 256, 16)
 
     def kernel(*refs):
         refs = list(refs)
-        lefts = [refs.pop(0) for _ in range(nc)]
-        rights = [refs.pop(0) for _ in range(nc)]
+        lefts = [refs.pop(0) for _ in range(nc * len(spans))]
+        rights = [refs.pop(0) for _ in range(nc * len(spans))]
         total_ref = refs.pop(0) if total is not None else None
         slopes_ref = refs.pop(0) if last else None
         out_ref = refs[1]
@@ -240,13 +258,19 @@
         out_ref[...] = value.astype(out_ref.dtype)
 
     tile = pl.BlockSpec((tall, hidden), lambda i: (i, 0))
-    operands = list(features) + list(weights)
-    specs = [pl.BlockSpec((tall, width), lambda i: (i, 0))] * nc
-    specs += [
-        pl.BlockSpec(
-            (hidden, width), lambda i: (0, first // width), pipeline_mode=pl.Buffered(1)
-        )
-    ] * nc
+    operands, specs = [], []
+    for ours, (width, _) in zip(features, spans):
+        operands += ours
+        specs += [pl.BlockSpec((tall, width), lambda i: (i, 0))] * nc
+    for width, first in spans:
+        operands += weights
+        specs += [
+            pl.BlockSpec(
+                (hidden, width),
+                lambda i, b=first // width: (0, b),
+                pipeline_mode=pl.Buffered(1),
+            )
+        ] * nc
     aliases = {}
     if total is not None:
         if not last:
@@ -275,7 +299,8 @@
     rows = shape[0]
     tall = divisor(rows, 384, 16)
     steps = rows // tall
-    count = arrived.shape[0] // rows - 1
+    whole_blocks = len(arrived) == 1 and arrived[0].shape[0] > rows
+    count = arrived[0].shape[0] // rows - 1 if whole_blocks else len(arrived)
 
     def kernel(table_ref, *refs):
         value = refs[0][...]
@@ -284,9 +309,11 @@
         refs[-2][...] = value
 
     def other(d):
+        if not whole_blocks:
+            return pl.BlockSpec((tall, width), lambda i, t: (i, 0))
         return pl.BlockSpec((tall, width), lambda i, t: (t[base + d] * steps + i, 0))
 
-    operands = [own] + [arrived] * count
+    operands = [own] + (arrived * count if whole_blocks else arrived)
     specs, aliases = [pl.BlockSpec((tall, width), lambda i, t: (i, 0))], {}
     specs += [other(d) for d in range(1, count + 1)]
     if whole is not None:
@@ -312,19 +339,24 @@
 def on_device(n, nc, nr, pre_act, w_out, grad_out):
     tokens = grad_out.shape[0] * n * nr
     factor = float(tokens) ** (-0.5)
-    col, rep = lax.axis_index("col"), lax.axis_index("rep")
+    row, col, rep = (lax.axis_index(axis) for axis in ("row", "col", "rep"))
+    local = grad_out.shape[0]
     rows, hidden = pre_act.shape
     part = hidden // nr
     shape = (part, grad_out.shape[1])
     spans = stages_of(grad_out.shape[1])
     count = len(spans)
+    groups = GROUPS if count == len(STAGES) else ((0,),)
     distances = list(range(nr - 1, -1, -1))
 
     def partner(d):
         return rep ^ d if nr & (nr - 1) == 0 else (rep + d) % nr
 
     places = [((j - col + nc) % nc) * rows for j in range(nc)]
-    table = jnp.stack([jnp.int32(v) for v in places + [partner(d) for d in range(nr)]])
+    ring = n <= RING_LIMIT and n % nc == 0 and count > 1
+    slots = [(row - s + 2 * n - col * (n // nc)) % n * local for s in range(n if ring else 0)]
+    partners = [partner(d) for d in range(nr)]
+    table = jnp.stack([jnp.int32(v) for v in places + partners + slots])
     token = jnp.zeros(TOKEN.shape, TOKEN.dtype)
     gathered, features, owns, arrived = {}, {}, {}, {}
     grad_act = grad_weight = None
@@ -336,33 +368,59 @@
         gathered[k] = lax.all_gather(columns, "row", axis=0, tiled=True)
         return token
 
-    token = gather(token, 0)
-    token = gather(token, 1)
+    def add_stage(token, k, whole):
+        return add_up(token, table, nc, owns[k], arrived[k], whole, shape, spans[k])
+
+    steps = []
+    token = gather(token, 1 if ring else 0)
+    if ring:
+        token, columns = cut(token, grad_out, *spans[0])
+        steps = [columns]
+    token = gather(token, 2 if ring else 1)
     token, act, slopes = activate(token, pre_act)
     acts = [act] + [swap(act, "col", nc, nc - j) for j in range(1, nc)]
     weights = [w_out] + [swap(w_out, "col", nc, nc - j) for j in range(1, nc)]
-    token = gather(token, 2)
+    for s in range(1, n if ring else 0):
+        piece = swap(steps[-1], "row", n, 1)
+        if s < n - 1:
+            token, piece = pass_on(token, piece)
+        steps.append(piece)
+    if not ring:
+        token = gather(token, 2)
 
     for k in range(count):
-        listed = [(gathered[k], j * rows, rows, j) for j in range(nc)]
+        if 0 < k < count - LATE:
+            token, grad_weight = add_stage(token, k - 1, grad_weight)
+        if ring and k == 0:
+            listed = [(steps[s], 0, local, nc + nr + s) for s in range(n)]
+        else:
+            listed = [(gathered[k], j * rows, rows, j) for j in range(nc)]
         token, sent, own, own_rows = terms(
-            token, table, listed, acts, part, distances, None, factor, True
+            token, table, nc, listed, acts, part, distances, None, factor, True
         )
         features[k] = [own_rows[0]] + [swap(own_rows[j], "col", nc, j) for j in range(1, nc)]
-        owns[k] = arrived[k] = own
-        if nr > 1:
-            arrived[k] = lax.all_to_all(sent, "rep", 0, 0, tiled=True)
-        token = gather(token, k + 3)
-        if k > 0:
-            token, grad_weight = add_up(
-                token, table, nc, owns[k - 1], arrived[k - 1], grad_weight, shape, spans[k - 1]
-            )
-        token, grad_act = products(
-            token, features[k], weights, spans[k], grad_act, slopes if k == count - 1 else None
-        )
-    token, grad_weight = add_up(
-        token, table, nc, owns[count - 1], arrived[count - 1], grad_weight, shape, spans[count - 1]
-    )
+        owns[k], arrived[k] = own, []
+        if nr > 1 and k < max(1, count - PERMUTED):
+            arrived[k] = [lax.all_to_all(sent, "rep", 0, 0, tiled=True)]
+        elif nr > 1:
+            arrived[k] = []
+            for d in distances[:-1]:
+                block = lax.dynamic_slice_in_dim(sent, partner(d) * part, part, 0)
+                way = [(p, p ^ d if nr & (nr - 1) == 0 else (p + d) % nr) for p in range(nr)]
+                arrived[k].append(lax.ppermute(block, "rep", way))
+        token = gather(token, k + (2 if ring else 3)) if not ring or k > 0 else token
+        for ks in groups:
+            if ks[-1] == k:
+                token, grad_act = products(
+                    token,
+                    [features[q] for q in ks],
+                    weights,
+                    [spans[q] for q in ks],
+                    grad_act,
+                    slopes if k == count - 1 else None,
+                )
+    for k in range(max(0, count - LATE - 1), count):
+        token, grad_weight = add_stage(token, k, grad_weight)
     return grad_act, grad_weight
 
 

time: 560 us -> 544 us (0.971)
  waiting for transfers between devices: 208 us -> 162 us
  starting transfers between devices: 20.7 us -> 52.2 us
  Pallas kernels: 313 us -> 304 us
  local copies, waits for them, and re-layouts: 3.57 us -> 10.2 us
    all_gather x4 -> x3, waiting for transfers between devices: 182 us -> 39.7 us  [gather(): gathered[k] = lax.all_gather(columns, 'row', axis=0, tiled=True)]
    ppermute x6 -> x9, waiting for transfers between devices: 21.5 us -> 81.8 us  [swap(): return lax.ppermute(x, axis, [(i, (i + step) % size) for i in range(size)])]
    ppermute x6 -> x9, starting transfers between devices: 1.27 us -> 33.7 us  [swap(): return lax.ppermute(x, axis, [(i, (i + step) % size) for i in range(size)])]
    all_to_all x4 -> x3, waiting for transfers between devices: 3.67 us -> 35.9 us  [on_device(): arrived[k] = [lax.all_to_all(sent, 'rep', 0, 0, tiled=True)]]
    pallas_call x4, Pallas kernels: 127 us -> 119 us  [products(): pl.pallas_call(kernel, out_shape=[jax.ShapeDtypeStruct((rows, hidden), ki...]
    all_to_all x4 -> x3, starting transfers between devices: 18.9 us -> 14.7 us  [on_device(): arrived[k] = [lax.all_to_all(sent, 'rep', 0, 0, tiled=True)]]
  transfers between devices with their start and end apart: 14 -> 18, of which waited for: 6 -> 11; matrix products, arithmetic and copies ran while one was open for 0% -> 1% of each run, Pallas kernels for 55% -> 55%
where the time goes in v3:
time: 544 us; the launch traced here: 542 us
  Pallas kernels  304 us (56%)
  waiting for transfers between devices  162 us (30%)
  starting transfers between devices  52.2 us (10%)
  between operations  13.9 us (3%)
  local copies, waits for them, and re-layouts  10.2 us (2%)
    pallas_call x4, Pallas kernels, terms(): pl.pallas_call(kernel, out_shape=shapes + [TOKEN], grid_spec=pltpu.Prefet...  124 us
    pallas_call x4, Pallas kernels, products(): pl.pallas_call(kernel, out_shape=[jax.ShapeDtypeStruct((rows, hidden), ki...  119 us
    ppermute x9, waiting for transfers between devices, swap(): return lax.ppermute(x, axis, [(i, (i + step) % size) for i in range(size)])  81.8 us
    all_gather x3, waiting for transfers between devices, gather(): gathered[k] = lax.all_gather(columns, 'row', axis=0, tiled=True)  39.7 us
    all_to_all x3, waiting for transfers between devices, on_device(): arrived[k] = [lax.all_to_all(sent, 'rep', 0, 0, tiled=True)]  35.9 us
    ppermute x9, starting transfers between devices, swap(): return lax.ppermute(x, axis, [(i, (i + step) % size) for i in range(size)])  33.7 us
    pallas_call x1, Pallas kernels, activate(): pl.pallas_call(kernel, out_shape=[jax.ShapeDtypeStruct((hidden, rows), jn...  28.3 us
    pallas_call x4, Pallas kernels, add_up(): pl.pallas_call(kernel, out_shape=[jax.ShapeDtypeStruct(shape, jnp.float32...  18.5 us
  transfers between devices with their start and end apart: 18, of which 11 were waited for; matrix products, arithmetic and copies ran while one was open for 1% of the time, Pallas kernels for 55%

profile of v3, /device:TPU:0, one launch (start us, length us, event | category | flops | bytes accessed | tf_op | source)
XLA Modules:
  0.0 542.2 jit_solution(4029559330154597394)
XLA Ops:
  7.2 0.0 all-gather.4.cloned.1.call-start
  7.2 0.6 broadcast_in_dim.3.token_ref
  7.8 4.0 shard_map.50
  11.8 0.0 all-gather.4.cloned.1.call-update
  11.8 0.0 all-gather.8.cloned.1.call-start
  11.9 0.5 collective-permute-start.5
  12.4 3.2 shard_map.51
  15.6 3.8 shard_map.52
  19.4 28.3 %shard_map.53 = (bf16[3072,2048]{1,0:T(8,128)(2,1)}, f32[2048,3072]{1,0:T(8,128)}, f32[8,128]{1,0:T(8,128)}) custom-call(bf16[2048,3072]{1,0:T(8,128)(2,1)} %x_ref.1, f32[8,128]{1,0:T(8,128)} %get-tuple-element.55.token_ref), custom_call_target="tpu_custom_call" | custom-call | tf_op jit(solution)/shard_map/pallas_call | solution.py:100
  47.6 0.1 collective-permute-start
  47.7 0.0 all-gather.8.cloned.1.call-update
  47.7 3.2 collective-permute-start.1
  50.9 25.8 %collective-permute-done.1.refs_0_ = bf16[1024,256]{1,0:T(8,128)(2,1)S(1)} collective-permute-done((bf16[1024,256]{1,0:T(8,128)(2,1)S(1)}, bf16[1024,256]{1,0:T(8,128)(2,1)S(1)}, u32[]{:S(2)}, u32[]{:S(2)}) %collective-permute-start.1) | collective-permute-done | bytes 524320 | tf_op jit(solution)/shard_map/ppermute | solution.py:52
  76.7 0.8 copy-done.3
  77.5 13.0 %collective-permute-start.2 = (bf16[1024,256]{1,0:T(8,128)(2,1)}, bf16[1024,256]{1,0:T(8,128)(2,1)S(1)}, u32[]{:S(2)}, u32[]{:S(2)}) collective-permute-start(bf16[1024,256]{1,0:T(8,128)(2,1)} %get-tuple-element.59.refs_1_), channel_id=1, source_target_pairs={{0,8},{8,16},{16,24},{24,0},{1,9},{9,17},{17,25},{25,1},{2,10},{10... | collective-permute-start | bytes 1572872 | tf_op jit(solution)/shard_map/ppermute | solution.py:52
  90.6 23.2 %collective-permute-done.2.refs_0_ = bf16[1024,256]{1,0:T(8,128)(2,1)S(1)} collective-permute-done((bf16[1024,256]{1,0:T(8,128)(2,1)}, bf16[1024,256]{1,0:T(8,128)(2,1)S(1)}, u32[]{:S(2)}, u32[]{:S(2)}) %collective-permute-start.2) | collective-permute-done | bytes 524320 | tf_op jit(solution)/shard_map/ppermute | solution.py:52
  113.8 0.8 copy-done.2
  114.6 16.6 %collective-permute-start.3 = (bf16[1024,256]{1,0:T(8,128)(2,1)}, bf16[1024,256]{1,0:T(8,128)(2,1)S(1)}, u32[]{:S(2)}, u32[]{:S(2)}) collective-permute-start(bf16[1024,256]{1,0:T(8,128)(2,1)} %get-tuple-element.61.refs_2_), channel_id=1, source_target_pairs={{0,8},{8,16},{16,24},{24,0},{1,9},{9,17},{17,25},{25,1},{2,10},{10... | collective-permute-start | bytes 1572872 | tf_op jit(solution)/shard_map/ppermute | solution.py:52
  131.2 0.7 stack.43.table_ref
  131.8 22.3 %collective-permute-done.3.refs_3_ = bf16[1024,256]{1,0:T(8,128)(2,1)S(1)} collective-permute-done((bf16[1024,256]{1,0:T(8,128)(2,1)}, bf16[1024,256]{1,0:T(8,128)(2,1)S(1)}, u32[]{:S(2)}, u32[]{:S(2)}) %collective-permute-start.3) | collective-permute-done | bytes 524320 | tf_op jit(solution)/shard_map/ppermute | solution.py:52
  154.1 0.0 collective-permute-done.refs_5_.refs_3_
  154.1 0.8 copy-done.7
  154.9 16.7 %shard_map.56 = (bf16[3072,256]{1,0:T(8,128)(2,1)}, f32[768,256]{1,0:T(8,128)}, bf16[2048,256]{1,0:T(8,128)(2,1)}, bf16[2048,256]{1,0:T(8,128)(2,1)}, f32[8,128]{1,0:T(8,128)}) custom-call(s32[10]{0:T(128)} %stack.43.table_ref, bf16[1024,256]{1,0:T(8,128)(2,1)} %get-tuple-element.57.refs_0_, bf16[1024,256]{1,0:T(8,128)(2,1)} %get-tuple-element.59.refs_1_, ...), custom_call_target="tpu_custom_call" | custom-call | tf_op jit(solution)/shard_map/pallas_call | solution.py:208
  171.6 3.7 all-to-all-start
  175.3 0.0 collective-permute-start.4
  175.3 2.9 collective-permute-done.4.refs_1_
  178.2 0.0 collective-permute-done.5.refs_3_
  178.2 1.0 copy-done.4
  179.2 13.1 %shard_map.57 = (f32[2048,3072]{1,0:T(8,128)}, f32[8,128]{1,0:T(8,128)}) custom-call(bf16[2048,256]{1,0:T(8,128)(2,1)} %get-tuple-element.65.refs_0_, bf16[2048,256]{1,0:T(8,128)(2,1)} %copy-done.4, bf16[3072,3072]{1,0:T(8,128)(2,1)} %refs_2_.7, bf16[3072,3072]{1,0:T(8,128)(2,1)} %collective-permute-done.5.refs_3_, f32[8,128]{1,0:T(8,128)} %get-tuple-element.67.refs_4_), custom_call_target="tpu_custom_call" | custom-call | tf_op jit(solution)/shard_map/pallas_call | solution.py:284
  192.2 1.2 all-to-all-done
  193.5 1.2 copy-done
  194.6 3.0 shard_map.58
  197.7 34.6 %all-gather.4.cloned.1.call-done.refs_0_.refs_1_ = bf16[4096,1280]{1,0:T(8,128)(2,1)} async-done(((bf16[1024,1280]{1,0:T(8,128)(2,1)}), bf16[4096,1280]{1,0:T(8,128)(2,1)}) %all-gather.4.cloned.1.call-update) | async-done | bytes 10485776 | tf_op jit(solution)/shard_map/all_gather | solution.py:368
  232.3 45.3 %shard_map.59 = (bf16[3072,1280]{1,0:T(8,128)(2,1)}, f32[768,1280]{1,0:T(8,128)}, bf16[2048,1280]{1,0:T(8,128)(2,1)}, bf16[2048,1280]{1,0:T(8,128)(2,1)}, f32[8,128]{1,0:T(8,128)}) custom-call(s32[10]{0:T(128)} %stack.43.table_ref, bf16[4096,1280]{1,0:T(8,128)(2,1)} %all-gather.4.cloned.1.call-done.refs_0_.refs_1_, ...), custom_call_target="tpu_custom_call" | custom-call | tf_op jit(solution)/shard_map/pallas_call | solution.py:208
  277.6 5.5 %all-to-all-start.1 = ((bf16[4,768,1280]{2,1,0:T(8,128)(2,1)}), bf16[4,768,1280]{2,1,0:T(8,128)(2,1)}, u32[]{:S(2)}, u32[]{:S(2)}) async-start(bf16[4,768,1280]{2,1,0:T(8,128)(2,1)} %bitcast.19), calls=%async_computation.1 | async-start | bytes 15728640 | tf_op jit(solution)/shard_map/all_to_all | solution.py:404
  283.1 0.2 all-gather.6.cloned.1.call-start
  283.4 0.1 collective-permute-start.6
  283.5 3.3 shard_map.60
  286.8 0.0 all-gather.6.cloned.1.call-update
  286.8 5.6 %collective-permute-done.6.refs_1_ = bf16[2048,1280]{1,0:T(8,128)(2,1)} collective-permute-done((bf16[2048,1280]{1,0:T(8,128)(2,1)}, bf16[2048,1280]{1,0:T(8,128)(2,1)}, u32[]{:S(2)}, u32[]{:S(2)}) %collective-permute-start.6) | collective-permute-done | bytes 5242912 | tf_op jit(solution)/shard_map/ppermute | solution.py:52
  292.4 43.2 %shard_map.61 = (f32[2048,3072]{1,0:T(8,128)}, f32[8,128]{1,0:T(8,128)}) custom-call(bf16[2048,1280]{1,0:T(8,128)(2,1)} %get-tuple-element.76.refs_0_, bf16[2048,1280]{1,0:T(8,128)(2,1)} %collective-permute-done.6.refs_1_, bf16[3072,3072]{1,0:T(8,128)(2,1)} %refs_2_.7, ...), custom_call_target="tpu_custom_call", output_to_operand_aliasing={{0}: (4, {})} | custom-call | tf_op jit(solution)/shard_map/pallas_call | solution.py:284
  335.6 34.6 %all-to-all-done.1 = bf16[4,768,1280]{2,1,0:T(8,128)(2,1)} async-done(((bf16[4,768,1280]{2,1,0:T(8,128)(2,1)}), bf16[4,768,1280]{2,1,0:T(8,128)(2,1)}, u32[]{:S(2)}, u32[]{:S(2)}) %all-to-all-start.1) | async-done | bytes 7864352 | tf_op jit(solution)/shard_map/all_to_all | solution.py:404
  370.2 6.3 %shard_map.62 = (f32[768,3072]{1,0:T(8,128)}, f32[8,128]{1,0:T(8,128)}) custom-call(s32[10]{0:T(128)} %stack.43.table_ref, f32[768,1280]{1,0:T(8,128)} %get-tuple-element.73.refs_0_, bf16[3072,1280]{1,0:T(8,128)(2,1)} %bitcast.13.refs_1_.refs_2_.refs_3_, bf16[3072,1280]{1,0:T(8,128)(2,1)} %bitcast.13.refs_1_.refs_2_.refs_3_, ...), custom_call_target="tpu_custom_call", output_to_operand_aliasing={{0}: (5, {})} | custom-call | tf_op jit(solution)/shard_map/pallas_call | solution.py:323
  376.6 5.1 all-gather.8.cloned.1.call-done.refs_0_.refs_1_
  381.7 39.3 %shard_map.63 = (bf16[3072,1024]{1,0:T(8,128)(2,1)}, f32[768,1024]{1,0:T(8,128)}, bf16[2048,1024]{1,0:T(8,128)(2,1)}, bf16[2048,1024]{1,0:T(8,128)(2,1)}, f32[8,128]{1,0:T(8,128)}) custom-call(s32[10]{0:T(128)} %stack.43.table_ref, bf16[4096,1024]{1,0:T(8,128)(2,1)} %all-gather.8.cloned.1.call-done.refs_0_.refs_1_, ...), custom_call_target="tpu_custom_call" | custom-call | tf_op jit(solution)/shard_map/pallas_call | solution.py:208
  421.0 0.1 collective-permute-start.7
  421.1 5.6 %all-to-all-start.2 = ((bf16[4,768,1024]{2,1,0:T(8,128)(2,1)}), bf16[4,768,1024]{2,1,0:T(8,128)(2,1)}, u32[]{:S(2)}, u32[]{:S(2)}) async-start(bf16[4,768,1024]{2,1,0:T(8,128)(2,1)} %bitcast.20), calls=%async_computation.2 | async-start | bytes 12582912 | tf_op jit(solution)/shard_map/all_to_all | solution.py:404
  426.7 1.9 collective-permute-done.7.refs_1_
  428.6 35.7 %shard_map.64 = (f32[2048,3072]{1,0:T(8,128)}, f32[8,128]{1,0:T(8,128)}) custom-call(bf16[2048,1024]{1,0:T(8,128)(2,1)} %get-tuple-element.82.refs_0_, bf16[2048,1024]{1,0:T(8,128)(2,1)} %collective-permute-done.7.refs_1_, bf16[3072,3072]{1,0:T(8,128)(2,1)} %refs_2_.7, ...), custom_call_target="tpu_custom_call", output_to_operand_aliasing={{0}: (4, {})} | custom-call | tf_op jit(solution)/shard_map/pallas_call | solution.py:284
  464.2 23.0 %shard_map.65 = (bf16[3072,512]{1,0:T(8,128)(2,1)}, f32[768,512]{1,0:T(8,128)}, bf16[2048,512]{1,0:T(8,128)(2,1)}, bf16[2048,512]{1,0:T(8,128)(2,1)}, f32[8,128]{1,0:T(8,128)}) custom-call(s32[10]{0:T(128)} %stack.43.table_ref, bf16[4096,512]{1,0:T(8,128)(2,1)} %all-gather.6.cloned.1.call-done.refs_0_.refs_1_, ...), custom_call_target="tpu_custom_call" | custom-call | tf_op jit(solution)/shard_map/pallas_call | solution.py:208
  487.2 0.2 collective-permute-start.8
  487.4 3.1 constant_dynamic-slice_fusion
  490.5 1.4 collective-permute-start.10
  491.9 1.5 collective-permute-start.11
  493.4 0.6 collective-permute-start.9
  494.0 0.0 collective-permute-done.8.refs_1_
  494.0 1.3 copy-done.1
  495.3 26.8 %shard_map.66 = (bf16[2048,3072]{1,0:T(8,128)(2,1)}, f32[8,128]{1,0:T(8,128)}) custom-call(bf16[2048,512]{1,0:T(8,128)(2,1)} %get-tuple-element.87.refs_0_, bf16[2048,512]{1,0:T(8,128)(2,1)} %copy-done.1, bf16[3072,3072]{1,0:T(8,128)(2,1)} %refs_2_.7, bf16[3072,3072]{1,0:T(8,128)(2,1)} %collective-permute-done.5.refs_3_, ...), custom_call_target="tpu_custom_call" | custom-call | tf_op jit(solution)/shard_map/pallas_call | solution.py:284
  522.1 0.0 all-to-all-done.2
  522.1 5.4 shard_map.67
  527.5 0.0 collective-permute-done.10.refs_2_
  527.5 0.0 collective-permute-done.11.refs_3_
  527.5 4.3 collective-permute-done.9.refs_1_
  531.8 3.8 shard_map.68
  (13 shorter events, 0.0 us)
Async XLA Ops:
  7.2 225.1 %all-gather.4.cloned.1.call-start = ((), (), s32[]{:S(2)}) async-start(), calls=%async_computation.3 | async-start | bytes 13107200 | tf_op jit(solution)/shard_map/all_gather | solution.py:368
  11.8 369.8 %all-gather.8.cloned.1.call-start = ((), (), s32[]{:S(2)}) async-start(), calls=%async_computation.5 | async-start | bytes 10485760 | tf_op jit(solution)/shard_map/all_gather | solution.py:368
  11.9 166.3 %collective-permute-start.5 = (bf16[3072,3072]{1,0:T(8,128)(2,1)}, bf16[3072,3072]{1,0:T(8,128)(2,1)}, u32[]{:S(2)}, u32[]{:S(2)}) collective-permute-start(bf16[3072,3072]{1,0:T(8,128)(2,1)} %refs_2_.7), channel_id=1, source_target_pairs={{0,4},{4,0},{1,5},{5,1},{2,6},{6,2},{3,7},{7,3},{8,12},{12,8},{9,1... | collective-permute-start | bytes 56623112 | tf_op jit(solution)/shard_map/ppermute | solution.py:52
  19.4 28.4 %copy-start.6 = (bf16[1024,256]{1,0:T(8,128)(2,1)S(1)}, bf16[1024,256]{1,0:T(8,128)(2,1)}, u32[]{:S(2)}) copy-start(bf16[1024,256]{1,0:T(8,128)(2,1)} %get-tuple-element.57.refs_0_) | copy-start | bytes 1572868
  47.6 106.5 %collective-permute-start = (bf16[3072,2048]{1,0:T(8,128)(2,1)}, bf16[3072,2048]{1,0:T(8,128)(2,1)}, u32[]{:S(2)}, u32[]{:S(2)}) collective-permute-start(bf16[3072,2048]{1,0:T(8,128)(2,1)} %get-tuple-element.56.refs_4_.refs_2_), channel_id=1, source_target_pairs={{0,4},{4,0},{1,5},{5,1},{2,6},{6,2},{3,7},{7,3},{8,12},{12,8},{9,1... | collective-permute-start | bytes 37748744 | tf_op jit(solution)/shard_map/ppermute | solution.py:52
  47.7 29.0 %collective-permute-start.1 = (bf16[1024,256]{1,0:T(8,128)(2,1)S(1)}, bf16[1024,256]{1,0:T(8,128)(2,1)S(1)}, u32[]{:S(2)}, u32[]{:S(2)}) collective-permute-start(bf16[1024,256]{1,0:T(8,128)(2,1)S(1)} %copy-done.6), channel_id=1, source_target_pairs={{0,8},{8,16},{16,24},{24,0},{1,9},{9,17},{17,25},{25,1},{2,10},{10... | collective-permute-start | bytes 1572872 | tf_op jit(solution)/shard_map/ppermute | solution.py:52
  76.7 0.8 copy-start.3
  77.5 36.2 %collective-permute-start.2 = (bf16[1024,256]{1,0:T(8,128)(2,1)}, bf16[1024,256]{1,0:T(8,128)(2,1)S(1)}, u32[]{:S(2)}, u32[]{:S(2)}) collective-permute-start(bf16[1024,256]{1,0:T(8,128)(2,1)} %get-tuple-element.59.refs_1_), channel_id=1, source_target_pairs={{0,8},{8,16},{16,24},{24,0},{1,9},{9,17},{17,25},{25,1},{2,10},{10... | collective-permute-start | bytes 1572872 | tf_op jit(solution)/shard_map/ppermute | solution.py:52
  113.8 0.8 copy-start.2
  114.6 39.5 %collective-permute-start.3 = (bf16[1024,256]{1,0:T(8,128)(2,1)}, bf16[1024,256]{1,0:T(8,128)(2,1)S(1)}, u32[]{:S(2)}, u32[]{:S(2)}) collective-permute-start(bf16[1024,256]{1,0:T(8,128)(2,1)} %get-tuple-element.61.refs_2_), channel_id=1, source_target_pairs={{0,8},{8,16},{16,24},{24,0},{1,9},{9,17},{17,25},{25,1},{2,10},{10... | collective-permute-start | bytes 1572872 | tf_op jit(solution)/shard_map/ppermute | solution.py:52
  154.1 0.8 copy-start.7
  171.6 21.8 %all-to-all-start = ((bf16[4,768,256]{2,1,0:T(8,128)(2,1)}), bf16[4,768,256]{2,1,0:T(8,128)(2,1)S(1)}, u32[]{:S(2)}, u32[]{:S(2)}) async-start(bf16[4,768,256]{2,1,0:T(8,128)(2,1)} %bitcast.21), calls=%async_computation | async-start | bytes 3145728 | tf_op jit(solution)/shard_map/all_to_all | solution.py:404
  175.3 2.9 collective-permute-start.4
  178.2 1.0 copy-start.4
  193.5 1.2 copy-start
  277.6 92.6 %all-to-all-start.1 = ((bf16[4,768,1280]{2,1,0:T(8,128)(2,1)}), bf16[4,768,1280]{2,1,0:T(8,128)(2,1)}, u32[]{:S(2)}, u32[]{:S(2)}) async-start(bf16[4,768,1280]{2,1,0:T(8,128)(2,1)} %bitcast.19), calls=%async_computation.1 | async-start | bytes 15728640 | tf_op jit(solution)/shard_map/all_to_all | solution.py:404
  283.1 181.1 %all-gather.6.cloned.1.call-start = ((), (), s32[]{:S(2)}) async-start(), calls=%async_computation.4 | async-start | bytes 5242880 | tf_op jit(solution)/shard_map/all_gather | solution.py:368
  283.4 9.1 %collective-permute-start.6 = (bf16[2048,1280]{1,0:T(8,128)(2,1)}, bf16[2048,1280]{1,0:T(8,128)(2,1)}, u32[]{:S(2)}, u32[]{:S(2)}) collective-permute-start(bf16[2048,1280]{1,0:T(8,128)(2,1)} %get-tuple-element.77), channel_id=1, source_target_pairs={{0,4},{4,0},{1,5},{5,1},{2,6},{6,2},{3,7},{7,3},{8,12},{12,8},{9,1... | collective-permute-start | bytes 15728648 | tf_op jit(solution)/shard_map/ppermute | solution.py:52
  421.0 7.6 %collective-permute-start.7 = (bf16[2048,1024]{1,0:T(8,128)(2,1)}, bf16[2048,1024]{1,0:T(8,128)(2,1)}, u32[]{:S(2)}, u32[]{:S(2)}) collective-permute-start(bf16[2048,1024]{1,0:T(8,128)(2,1)} %get-tuple-element.83), channel_id=1, source_target_pairs={{0,4},{4,0},{1,5},{5,1},{2,6},{6,2},{3,7},{7,3},{8,12},{12,8},{9,1... | collective-permute-start | bytes 12582920 | tf_op jit(solution)/shard_map/ppermute | solution.py:52
  421.1 101.0 %all-to-all-start.2 = ((bf16[4,768,1024]{2,1,0:T(8,128)(2,1)}), bf16[4,768,1024]{2,1,0:T(8,128)(2,1)}, u32[]{:S(2)}, u32[]{:S(2)}) async-start(bf16[4,768,1024]{2,1,0:T(8,128)(2,1)} %bitcast.20), calls=%async_computation.2 | async-start | bytes 12582912 | tf_op jit(solution)/shard_map/all_to_all | solution.py:404
  487.2 6.8 %collective-permute-start.8 = (bf16[2048,512]{1,0:T(8,128)(2,1)}, bf16[2048,512]{1,0:T(8,128)(2,1)S(1)}, u32[]{:S(2)}, u32[]{:S(2)}) collective-permute-start(bf16[2048,512]{1,0:T(8,128)(2,1)} %get-tuple-element.88), channel_id=1, source_target_pairs={{0,4},{4,0},{1,5},{5,1},{2,6},{6,2},{3,7},{7,3},{8,12},{12,8},{9,1... | collective-permute-start | bytes 6291464 | tf_op jit(solution)/shard_map/ppermute | solution.py:52
  490.5 37.0 %collective-permute-start.10 = (bf16[768,512]{1,0:T(8,128)(2,1)}, bf16[768,512]{1,0:T(8,128)(2,1)S(1)}, u32[]{:S(2)}, u32[]{:S(2)}) collective-permute-start(bf16[768,512]{1,0:T(8,128)(2,1)} %get-tuple-element.103), channel_id=1, source_target_pairs={{0,2},{1,3},{2,0},{3,1},{4,6},{5,7},{6,4},{7,5},{8,10},{9,11},{10,... | collective-permute-start | bytes 2359304 | tf_op jit(solution)/shard_map/ppermute | solution.py:410
  491.9 35.6 %collective-permute-start.11 = (bf16[768,512]{1,0:T(8,128)(2,1)}, bf16[768,512]{1,0:T(8,128)(2,1)}, u32[]{:S(2)}, u32[]{:S(2)}) collective-permute-start(bf16[768,512]{1,0:T(8,128)(2,1)} %get-tuple-element.102), channel_id=1, source_target_pairs={{0,1},{1,0},{2,3},{3,2},{4,5},{5,4},{6,7},{7,6},{8,9},{9,8},{10,11... | collective-permute-start | bytes 2359304 | tf_op jit(solution)/shard_map/ppermute | solution.py:410
  493.4 38.4 %collective-permute-start.9 = (bf16[768,512]{1,0:T(8,128)(2,1)}, bf16[768,512]{1,0:T(8,128)(2,1)}, u32[]{:S(2)}, u32[]{:S(2)}) collective-permute-start(bf16[768,512]{1,0:T(8,128)(2,1)} %get-tuple-element.104), channel_id=1, source_target_pairs={{0,3},{1,2},{2,1},{3,0},{4,7},{5,6},{6,5},{7,4},{8,11},{9,10},{10,... | collective-permute-start | bytes 2359304 | tf_op jit(solution)/shard_map/ppermute | solution.py:410
  494.0 1.3 copy-start.1
  527.5 4.3 copy-start.5
Sparse Core Ops, SparseCore 0:
  12.0 220.2 all-gather.3
  233.8 147.7 all-gather.7
  383.2 78.9 all-gather.5

commit v4 on v3

--- a/solution.py
+++ b/solution.py
@@ -404,7 +404,7 @@
             arrived[k] = [lax.all_to_all(sent, "rep", 0, 0, tiled=True)]
         elif nr > 1:
             arrived[k] = []
-            for d in distances[:-1]:
+            for d in reversed(distances[:-1]):
                 block = lax.dynamic_slice_in_dim(sent, partner(d) * part, part, 0)
                 way = [(p, p ^ d if nr & (nr - 1) == 0 else (p + d) % nr) for p in range(nr)]
                 arrived[k].append(lax.ppermute(block, "rep", way))

time: 544 us -> 543 us (level)
  transfers between devices with their start and end apart: 18 -> 18, of which waited for: 11 -> 12; matrix products, arithmetic and copies ran while one was open for 1% -> 1% of each run, Pallas kernels for 55% -> 55%
where the time goes in v4:
time: 543 us; the launch traced here: 542 us
  Pallas kernels  304 us (56%)
  waiting for transfers between devices  161 us (30%)
  starting transfers between devices  52.2 us (10%)
  between operations  13.8 us (3%)
  local copies, waits for them, and re-layouts  11 us (2%)
    pallas_call x4, Pallas kernels, terms(): pl.pallas_call(kernel, out_shape=shapes + [TOKEN], grid_spec=pltpu.Prefet...  124 us
    pallas_call x4, Pallas kernels, products(): pl.pallas_call(kernel, out_shape=[jax.ShapeDtypeStruct((rows, hidden), ki...  119 us
    ppermute x9, waiting for transfers between devices, swap(): return lax.ppermute(x, axis, [(i, (i + step) % size) for i in range(size)])  81.8 us
    all_gather x3, waiting for transfers between devices, gather(): gathered[k] = lax.all_gather(columns, 'row', axis=0, tiled=True)  39.7 us
    all_to_all x3, waiting for transfers between devices, on_device(): arrived[k] = [lax.all_to_all(sent, 'rep', 0, 0, tiled=True)]  35.8 us
    ppermute x9, starting transfers between devices, swap(): return lax.ppermute(x, axis, [(i, (i + step) % size) for i in range(size)])  33.7 us
    pallas_call x1, Pallas kernels, activate(): pl.pallas_call(kernel, out_shape=[jax.ShapeDtypeStruct((hidden, rows), jn...  28.3 us
    pallas_call x4, Pallas kernels, add_up(): pl.pallas_call(kernel, out_shape=[jax.ShapeDtypeStruct(shape, jnp.float32...  18.5 us
  transfers between devices with their start and end apart: 18, of which 12 were waited for; matrix products, arithmetic and copies ran while one was open for 1% of the time, Pallas kernels for 55%

profile of v4, /device:TPU:0, one launch (start us, length us, event | category | flops | bytes accessed | tf_op | source)
XLA Modules:
  0.0 542.0 jit_solution(3222294813790696125)
XLA Ops:
  7.2 0.0 all-gather.4.cloned.1.call-start
  7.2 0.6 broadcast_in_dim.3.token_ref
  7.8 4.0 shard_map.50
  11.8 0.0 all-gather.4.cloned.1.call-update
  11.8 0.0 all-gather.8.cloned.1.call-start
  11.9 0.5 collective-permute-start.5
  12.4 3.2 shard_map.51
  15.6 3.8 shard_map.52
  19.4 28.3 %shard_map.53 = (bf16[3072,2048]{1,0:T(8,128)(2,1)}, f32[2048,3072]{1,0:T(8,128)}, f32[8,128]{1,0:T(8,128)}) custom-call(bf16[2048,3072]{1,0:T(8,128)(2,1)} %x_ref.1, f32[8,128]{1,0:T(8,128)} %get-tuple-element.55.token_ref), custom_call_target="tpu_custom_call" | custom-call | tf_op jit(solution)/shard_map/pallas_call | solution.py:100
  47.6 0.1 collective-permute-start
  47.7 0.0 all-gather.8.cloned.1.call-update
  47.7 3.2 collective-permute-start.1
  50.9 25.8 %collective-permute-done.1.refs_0_ = bf16[1024,256]{1,0:T(8,128)(2,1)S(1)} collective-permute-done((bf16[1024,256]{1,0:T(8,128)(2,1)S(1)}, bf16[1024,256]{1,0:T(8,128)(2,1)S(1)}, u32[]{:S(2)}, u32[]{:S(2)}) %collective-permute-start.1) | collective-permute-done | bytes 524320 | tf_op jit(solution)/shard_map/ppermute | solution.py:52
  76.7 0.8 copy-done.3
  77.5 13.0 %collective-permute-start.2 = (bf16[1024,256]{1,0:T(8,128)(2,1)}, bf16[1024,256]{1,0:T(8,128)(2,1)S(1)}, u32[]{:S(2)}, u32[]{:S(2)}) collective-permute-start(bf16[1024,256]{1,0:T(8,128)(2,1)} %get-tuple-element.59.refs_1_), channel_id=1, source_target_pairs={{0,8},{8,16},{16,24},{24,0},{1,9},{9,17},{17,25},{25,1},{2,10},{10... | collective-permute-start | bytes 1572872 | tf_op jit(solution)/shard_map/ppermute | solution.py:52
  90.6 23.2 %collective-permute-done.2.refs_0_ = bf16[1024,256]{1,0:T(8,128)(2,1)S(1)} collective-permute-done((bf16[1024,256]{1,0:T(8,128)(2,1)}, bf16[1024,256]{1,0:T(8,128)(2,1)S(1)}, u32[]{:S(2)}, u32[]{:S(2)}) %collective-permute-start.2) | collective-permute-done | bytes 524320 | tf_op jit(solution)/shard_map/ppermute | solution.py:52
  113.8 0.8 copy-done.2
  114.6 16.6 %collective-permute-start.3 = (bf16[1024,256]{1,0:T(8,128)(2,1)}, bf16[1024,256]{1,0:T(8,128)(2,1)S(1)}, u32[]{:S(2)}, u32[]{:S(2)}) collective-permute-start(bf16[1024,256]{1,0:T(8,128)(2,1)} %get-tuple-element.61.refs_2_), channel_id=1, source_target_pairs={{0,8},{8,16},{16,24},{24,0},{1,9},{9,17},{17,25},{25,1},{2,10},{10... | collective-permute-start | bytes 1572872 | tf_op jit(solution)/shard_map/ppermute | solution.py:52
  131.2 0.7 stack.43.table_ref
  131.8 22.3 %collective-permute-done.3.refs_3_ = bf16[1024,256]{1,0:T(8,128)(2,1)S(1)} collective-permute-done((bf16[1024,256]{1,0:T(8,128)(2,1)}, bf16[1024,256]{1,0:T(8,128)(2,1)S(1)}, u32[]{:S(2)}, u32[]{:S(2)}) %collective-permute-start.3) | collective-permute-done | bytes 524320 | tf_op jit(solution)/shard_map/ppermute | solution.py:52
  154.1 0.0 collective-permute-done.refs_5_.refs_3_
  154.1 0.8 copy-done.7
  154.9 16.7 %shard_map.56 = (bf16[3072,256]{1,0:T(8,128)(2,1)}, f32[768,256]{1,0:T(8,128)}, bf16[2048,256]{1,0:T(8,128)(2,1)}, bf16[2048,256]{1,0:T(8,128)(2,1)}, f32[8,128]{1,0:T(8,128)}) custom-call(s32[10]{0:T(128)} %stack.43.table_ref, bf16[1024,256]{1,0:T(8,128)(2,1)} %get-tuple-element.57.refs_0_, bf16[1024,256]{1,0:T(8,128)(2,1)} %get-tuple-element.59.refs_1_, ...), custom_call_target="tpu_custom_call" | custom-call | tf_op jit(solution)/shard_map/pallas_call | solution.py:208
  171.6 3.7 all-to-all-start
  175.3 0.0 collective-permute-start.4
  175.3 2.9 collective-permute-done.4.refs_1_
  178.2 0.0 collective-permute-done.5.refs_3_
  178.2 1.0 copy-done.4
  179.2 13.1 %shard_map.57 = (f32[2048,3072]{1,0:T(8,128)}, f32[8,128]{1,0:T(8,128)}) custom-call(bf16[2048,256]{1,0:T(8,128)(2,1)} %get-tuple-element.65.refs_0_, bf16[2048,256]{1,0:T(8,128)(2,1)} %copy-done.4, bf16[3072,3072]{1,0:T(8,128)(2,1)} %refs_2_.7, bf16[3072,3072]{1,0:T(8,128)(2,1)} %collective-permute-done.5.refs_3_, f32[8,128]{1,0:T(8,128)} %get-tuple-element.67.refs_4_), custom_call_target="tpu_custom_call" | custom-call | tf_op jit(solution)/shard_map/pallas_call | solution.py:284
  192.2 1.2 all-to-all-done
  193.5 1.2 copy-done
  194.6 3.0 shard_map.58
  197.7 34.6 %all-gather.4.cloned.1.call-done.refs_0_.refs_1_ = bf16[4096,1280]{1,0:T(8,128)(2,1)} async-done(((bf16[1024,1280]{1,0:T(8,128)(2,1)}), bf16[4096,1280]{1,0:T(8,128)(2,1)}) %all-gather.4.cloned.1.call-update) | async-done | bytes 10485776 | tf_op jit(solution)/shard_map/all_gather | solution.py:368
  232.3 45.3 %shard_map.59 = (bf16[3072,1280]{1,0:T(8,128)(2,1)}, f32[768,1280]{1,0:T(8,128)}, bf16[2048,1280]{1,0:T(8,128)(2,1)}, bf16[2048,1280]{1,0:T(8,128)(2,1)}, f32[8,128]{1,0:T(8,128)}) custom-call(s32[10]{0:T(128)} %stack.43.table_ref, bf16[4096,1280]{1,0:T(8,128)(2,1)} %all-gather.4.cloned.1.call-done.refs_0_.refs_1_, ...), custom_call_target="tpu_custom_call" | custom-call | tf_op jit(solution)/shard_map/pallas_call | solution.py:208
  277.6 5.5 %all-to-all-start.1 = ((bf16[4,768,1280]{2,1,0:T(8,128)(2,1)}), bf16[4,768,1280]{2,1,0:T(8,128)(2,1)}, u32[]{:S(2)}, u32[]{:S(2)}) async-start(bf16[4,768,1280]{2,1,0:T(8,128)(2,1)} %bitcast.19), calls=%async_computation.1 | async-start | bytes 15728640 | tf_op jit(solution)/shard_map/all_to_all | solution.py:404
  283.1 0.2 all-gather.6.cloned.1.call-start
  283.4 0.1 collective-permute-start.6
  283.5 3.3 shard_map.60
  286.8 0.0 all-gather.6.cloned.1.call-update
  286.8 5.6 %collective-permute-done.6.refs_1_ = bf16[2048,1280]{1,0:T(8,128)(2,1)} collective-permute-done((bf16[2048,1280]{1,0:T(8,128)(2,1)}, bf16[2048,1280]{1,0:T(8,128)(2,1)}, u32[]{:S(2)}, u32[]{:S(2)}) %collective-permute-start.6) | collective-permute-done | bytes 5242912 | tf_op jit(solution)/shard_map/ppermute | solution.py:52
  292.4 43.2 %shard_map.61 = (f32[2048,3072]{1,0:T(8,128)}, f32[8,128]{1,0:T(8,128)}) custom-call(bf16[2048,1280]{1,0:T(8,128)(2,1)} %get-tuple-element.76.refs_0_, bf16[2048,1280]{1,0:T(8,128)(2,1)} %collective-permute-done.6.refs_1_, bf16[3072,3072]{1,0:T(8,128)(2,1)} %refs_2_.7, ...), custom_call_target="tpu_custom_call", output_to_operand_aliasing={{0}: (4, {})} | custom-call | tf_op jit(solution)/shard_map/pallas_call | solution.py:284
  335.6 34.6 %all-to-all-done.1 = bf16[4,768,1280]{2,1,0:T(8,128)(2,1)} async-done(((bf16[4,768,1280]{2,1,0:T(8,128)(2,1)}), bf16[4,768,1280]{2,1,0:T(8,128)(2,1)}, u32[]{:S(2)}, u32[]{:S(2)}) %all-to-all-start.1) | async-done | bytes 7864352 | tf_op jit(solution)/shard_map/all_to_all | solution.py:404
  370.2 6.3 %shard_map.62 = (f32[768,3072]{1,0:T(8,128)}, f32[8,128]{1,0:T(8,128)}) custom-call(s32[10]{0:T(128)} %stack.43.table_ref, f32[768,1280]{1,0:T(8,128)} %get-tuple-element.73.refs_0_, bf16[3072,1280]{1,0:T(8,128)(2,1)} %bitcast.13.refs_1_.refs_2_.refs_3_, bf16[3072,1280]{1,0:T(8,128)(2,1)} %bitcast.13.refs_1_.refs_2_.refs_3_, ...), custom_call_target="tpu_custom_call", output_to_operand_aliasing={{0}: (5, {})} | custom-call | tf_op jit(solution)/shard_map/pallas_call | solution.py:323
  376.6 5.1 all-gather.8.cloned.1.call-done.refs_0_.refs_1_
  381.7 39.3 %shard_map.63 = (bf16[3072,1024]{1,0:T(8,128)(2,1)}, f32[768,1024]{1,0:T(8,128)}, bf16[2048,1024]{1,0:T(8,128)(2,1)}, bf16[2048,1024]{1,0:T(8,128)(2,1)}, f32[8,128]{1,0:T(8,128)}) custom-call(s32[10]{0:T(128)} %stack.43.table_ref, bf16[4096,1024]{1,0:T(8,128)(2,1)} %all-gather.8.cloned.1.call-done.refs_0_.refs_1_, ...), custom_call_target="tpu_custom_call" | custom-call | tf_op jit(solution)/shard_map/pallas_call | solution.py:208
  421.0 0.1 collective-permute-start.7
  421.1 5.6 %all-to-all-start.2 = ((bf16[4,768,1024]{2,1,0:T(8,128)(2,1)}), bf16[4,768,1024]{2,1,0:T(8,128)(2,1)}, u32[]{:S(2)}, u32[]{:S(2)}) async-start(bf16[4,768,1024]{2,1,0:T(8,128)(2,1)} %bitcast.20), calls=%async_computation.2 | async-start | bytes 12582912 | tf_op jit(solution)/shard_map/all_to_all | solution.py:404
  426.7 1.9 collective-permute-done.7.refs_1_
  428.6 35.7 %shard_map.64 = (f32[2048,3072]{1,0:T(8,128)}, f32[8,128]{1,0:T(8,128)}) custom-call(bf16[2048,1024]{1,0:T(8,128)(2,1)} %get-tuple-element.82.refs_0_, bf16[2048,1024]{1,0:T(8,128)(2,1)} %collective-permute-done.7.refs_1_, bf16[3072,3072]{1,0:T(8,128)(2,1)} %refs_2_.7, ...), custom_call_target="tpu_custom_call", output_to_operand_aliasing={{0}: (4, {})} | custom-call | tf_op jit(solution)/shard_map/pallas_call | solution.py:284
  464.2 23.0 %shard_map.65 = (bf16[3072,512]{1,0:T(8,128)(2,1)}, f32[768,512]{1,0:T(8,128)}, bf16[2048,512]{1,0:T(8,128)(2,1)}, bf16[2048,512]{1,0:T(8,128)(2,1)}, f32[8,128]{1,0:T(8,128)}) custom-call(s32[10]{0:T(128)} %stack.43.table_ref, bf16[4096,512]{1,0:T(8,128)(2,1)} %all-gather.6.cloned.1.call-done.refs_0_.refs_1_, ...), custom_call_target="tpu_custom_call" | custom-call | tf_op jit(solution)/shard_map/pallas_call | solution.py:208
  487.2 0.2 collective-permute-start.8
  487.4 3.1 constant_dynamic-slice_fusion
  490.5 1.4 collective-permute-start.10
  491.9 1.6 collective-permute-start.11
  493.5 0.5 collective-permute-start.9
  494.0 0.0 collective-permute-done.8.refs_1_
  494.0 1.3 copy-done.1
  495.3 26.8 %shard_map.66 = (bf16[2048,3072]{1,0:T(8,128)(2,1)}, f32[8,128]{1,0:T(8,128)}) custom-call(bf16[2048,512]{1,0:T(8,128)(2,1)} %get-tuple-element.87.refs_0_, bf16[2048,512]{1,0:T(8,128)(2,1)} %copy-done.1, bf16[3072,3072]{1,0:T(8,128)(2,1)} %refs_2_.7, bf16[3072,3072]{1,0:T(8,128)(2,1)} %collective-permute-done.5.refs_3_, ...), custom_call_target="tpu_custom_call" | custom-call | tf_op jit(solution)/shard_map/pallas_call | solution.py:284
  522.1 5.4 shard_map.67
  527.5 3.3 collective-permute-done.10.refs_2_
  530.8 0.0 collective-permute-done.11.refs_3_
  530.8 0.2 collective-permute-done.9.refs_1_
  531.0 0.7 copy-done.5
  531.7 3.8 shard_map.68
  (13 shorter events, 0.0 us)
Async XLA Ops:
  7.2 225.1 %all-gather.4.cloned.1.call-start = ((), (), s32[]{:S(2)}) async-start(), calls=%async_computation.3 | async-start | bytes 13107200 | tf_op jit(solution)/shard_map/all_gather | solution.py:368
  11.8 369.8 %all-gather.8.cloned.1.call-start = ((), (), s32[]{:S(2)}) async-start(), calls=%async_computation.5 | async-start | bytes 10485760 | tf_op jit(solution)/shard_map/all_gather | solution.py:368
  11.9 166.3 %collective-permute-start.5 = (bf16[3072,3072]{1,0:T(8,128)(2,1)}, bf16[3072,3072]{1,0:T(8,128)(2,1)}, u32[]{:S(2)}, u32[]{:S(2)}) collective-permute-start(bf16[3072,3072]{1,0:T(8,128)(2,1)} %refs_2_.7), channel_id=1, source_target_pairs={{0,4},{4,0},{1,5},{5,1},{2,6},{6,2},{3,7},{7,3},{8,12},{12,8},{9,1... | collective-permute-start | bytes 56623112 | tf_op jit(solution)/shard_map/ppermute | solution.py:52
  19.4 28.4 %copy-start.6 = (bf16[1024,256]{1,0:T(8,128)(2,1)S(1)}, bf16[1024,256]{1,0:T(8,128)(2,1)}, u32[]{:S(2)}) copy-start(bf16[1024,256]{1,0:T(8,128)(2,1)} %get-tuple-element.57.refs_0_) | copy-start | bytes 1572868
  47.6 106.5 %collective-permute-start = (bf16[3072,2048]{1,0:T(8,128)(2,1)}, bf16[3072,2048]{1,0:T(8,128)(2,1)}, u32[]{:S(2)}, u32[]{:S(2)}) collective-permute-start(bf16[3072,2048]{1,0:T(8,128)(2,1)} %get-tuple-element.56.refs_4_.refs_2_), channel_id=1, source_target_pairs={{0,4},{4,0},{1,5},{5,1},{2,6},{6,2},{3,7},{7,3},{8,12},{12,8},{9,1... | collective-permute-start | bytes 37748744 | tf_op jit(solution)/shard_map/ppermute | solution.py:52
  47.7 29.0 %collective-permute-start.1 = (bf16[1024,256]{1,0:T(8,128)(2,1)S(1)}, bf16[1024,256]{1,0:T(8,128)(2,1)S(1)}, u32[]{:S(2)}, u32[]{:S(2)}) collective-permute-start(bf16[1024,256]{1,0:T(8,128)(2,1)S(1)} %copy-done.6), channel_id=1, source_target_pairs={{0,8},{8,16},{16,24},{24,0},{1,9},{9,17},{17,25},{25,1},{2,10},{10... | collective-permute-start | bytes 1572872 | tf_op jit(solution)/shard_map/ppermute | solution.py:52
  76.7 0.8 copy-start.3
  77.5 36.2 %collective-permute-start.2 = (bf16[1024,256]{1,0:T(8,128)(2,1)}, bf16[1024,256]{1,0:T(8,128)(2,1)S(1)}, u32[]{:S(2)}, u32[]{:S(2)}) collective-permute-start(bf16[1024,256]{1,0:T(8,128)(2,1)} %get-tuple-element.59.refs_1_), channel_id=1, source_target_pairs={{0,8},{8,16},{16,24},{24,0},{1,9},{9,17},{17,25},{25,1},{2,10},{10... | collective-permute-start | bytes 1572872 | tf_op jit(solution)/shard_map/ppermute | solution.py:52
  113.8 0.8 copy-start.2
  114.6 39.5 %collective-permute-start.3 = (bf16[1024,256]{1,0:T(8,128)(2,1)}, bf16[1024,256]{1,0:T(8,128)(2,1)S(1)}, u32[]{:S(2)}, u32[]{:S(2)}) collective-permute-start(bf16[1024,256]{1,0:T(8,128)(2,1)} %get-tuple-element.61.refs_2_), channel_id=1, source_target_pairs={{0,8},{8,16},{16,24},{24,0},{1,9},{9,17},{17,25},{25,1},{2,10},{10... | collective-permute-start | bytes 1572872 | tf_op jit(solution)/shard_map/ppermute | solution.py:52
  154.1 0.8 copy-start.7
  171.6 21.8 %all-to-all-start = ((bf16[4,768,256]{2,1,0:T(8,128)(2,1)}), bf16[4,768,256]{2,1,0:T(8,128)(2,1)S(1)}, u32[]{:S(2)}, u32[]{:S(2)}) async-start(bf16[4,768,256]{2,1,0:T(8,128)(2,1)} %bitcast.21), calls=%async_computation | async-start | bytes 3145728 | tf_op jit(solution)/shard_map/all_to_all | solution.py:404
  175.3 2.9 collective-permute-start.4
  178.2 1.0 copy-start.4
  193.5 1.2 copy-start
  277.6 92.6 %all-to-all-start.1 = ((bf16[4,768,1280]{2,1,0:T(8,128)(2,1)}), bf16[4,768,1280]{2,1,0:T(8,128)(2,1)}, u32[]{:S(2)}, u32[]{:S(2)}) async-start(bf16[4,768,1280]{2,1,0:T(8,128)(2,1)} %bitcast.19), calls=%async_computation.1 | async-start | bytes 15728640 | tf_op jit(solution)/shard_map/all_to_all | solution.py:404
  283.1 181.1 %all-gather.6.cloned.1.call-start = ((), (), s32[]{:S(2)}) async-start(), calls=%async_computation.4 | async-start | bytes 5242880 | tf_op jit(solution)/shard_map/all_gather | solution.py:368
  283.4 9.1 %collective-permute-start.6 = (bf16[2048,1280]{1,0:T(8,128)(2,1)}, bf16[2048,1280]{1,0:T(8,128)(2,1)}, u32[]{:S(2)}, u32[]{:S(2)}) collective-permute-start(bf16[2048,1280]{1,0:T(8,128)(2,1)} %get-tuple-element.77), channel_id=1, source_target_pairs={{0,4},{4,0},{1,5},{5,1},{2,6},{6,2},{3,7},{7,3},{8,12},{12,8},{9,1... | collective-permute-start | bytes 15728648 | tf_op jit(solution)/shard_map/ppermute | solution.py:52
  421.0 7.6 %collective-permute-start.7 = (bf16[2048,1024]{1,0:T(8,128)(2,1)}, bf16[2048,1024]{1,0:T(8,128)(2,1)}, u32[]{:S(2)}, u32[]{:S(2)}) collective-permute-start(bf16[2048,1024]{1,0:T(8,128)(2,1)} %get-tuple-element.83), channel_id=1, source_target_pairs={{0,4},{4,0},{1,5},{5,1},{2,6},{6,2},{3,7},{7,3},{8,12},{12,8},{9,1... | collective-permute-start | bytes 12582920 | tf_op jit(solution)/shard_map/ppermute | solution.py:52
  421.1 101.0 %all-to-all-start.2 = ((bf16[4,768,1024]{2,1,0:T(8,128)(2,1)}), bf16[4,768,1024]{2,1,0:T(8,128)(2,1)}, u32[]{:S(2)}, u32[]{:S(2)}) async-start(bf16[4,768,1024]{2,1,0:T(8,128)(2,1)} %bitcast.20), calls=%async_computation.2 | async-start | bytes 12582912 | tf_op jit(solution)/shard_map/all_to_all | solution.py:404
  487.2 6.8 %collective-permute-start.8 = (bf16[2048,512]{1,0:T(8,128)(2,1)}, bf16[2048,512]{1,0:T(8,128)(2,1)S(1)}, u32[]{:S(2)}, u32[]{:S(2)}) collective-permute-start(bf16[2048,512]{1,0:T(8,128)(2,1)} %get-tuple-element.88), channel_id=1, source_target_pairs={{0,4},{4,0},{1,5},{5,1},{2,6},{6,2},{3,7},{7,3},{8,12},{12,8},{9,1... | collective-permute-start | bytes 6291464 | tf_op jit(solution)/shard_map/ppermute | solution.py:52
  490.5 40.3 %collective-permute-start.10 = (bf16[768,512]{1,0:T(8,128)(2,1)}, bf16[768,512]{1,0:T(8,128)(2,1)S(1)}, u32[]{:S(2)}, u32[]{:S(2)}) collective-permute-start(bf16[768,512]{1,0:T(8,128)(2,1)} %get-tuple-element.103), channel_id=1, source_target_pairs={{0,2},{1,3},{2,0},{3,1},{4,6},{5,7},{6,4},{7,5},{8,10},{9,11},{10,... | collective-permute-start | bytes 2359304 | tf_op jit(solution)/shard_map/ppermute | solution.py:410
  491.9 38.9 %collective-permute-start.11 = (bf16[768,512]{1,0:T(8,128)(2,1)}, bf16[768,512]{1,0:T(8,128)(2,1)}, u32[]{:S(2)}, u32[]{:S(2)}) collective-permute-start(bf16[768,512]{1,0:T(8,128)(2,1)} %get-tuple-element.102), channel_id=1, source_target_pairs={{0,3},{1,2},{2,1},{3,0},{4,7},{5,6},{6,5},{7,4},{8,11},{9,10},{10,... | collective-permute-start | bytes 2359304 | tf_op jit(solution)/shard_map/ppermute | solution.py:410
  493.5 37.4 %collective-permute-start.9 = (bf16[768,512]{1,0:T(8,128)(2,1)}, bf16[768,512]{1,0:T(8,128)(2,1)}, u32[]{:S(2)}, u32[]{:S(2)}) collective-permute-start(bf16[768,512]{1,0:T(8,128)(2,1)} %get-tuple-element.104), channel_id=1, source_target_pairs={{0,1},{1,0},{2,3},{3,2},{4,5},{5,4},{6,7},{7,6},{8,9},{9,8},{10,11... | collective-permute-start | bytes 2359304 | tf_op jit(solution)/shard_map/ppermute | solution.py:410
  494.0 1.3 copy-start.1
  530.8 0.9 copy-start.5
Sparse Core Ops, SparseCore 0:
  12.0 220.2 all-gather.3
  233.8 147.7 all-gather.7
  383.2 78.9 all-gather.5
